TPU v7x, 32 devices: a whole 2x2x4 slice. The times are simulated.
32 devices in a mesh: dp: 8 (over z, y), head: 4 (over x, core).
Axes of the slice: x: 2, y: 2, z: 4, core: 2. Of those that a mesh axis runs over, the one named last changes fastest.
Arguments:
- tokens: bfloat16 [16384, 768], P(('dp', 'head')), may hold values from -6 to 6
- seq_len: int32 [128], P('dp'), may hold values from 128 to 512, as said below
- norm1_gain: float32 [768], replicated, may hold values from 0.25 to 1.75
- norm1_bias: float32 [768], replicated, may hold values from -1.75 to 1.75
- f1_weight: bfloat16 [12, 768, 768], P('head'), may hold values from -0.21875 to 0.21875
- f1_bias: float32 [12, 768], P('head'), may hold values from -3 to 3
- f2_weight: bfloat16 [12, 768, 512], P('head'), may hold values from -0.4375 to 0.4375
- f2_bias: float32 [12, 512], P('head'), may hold values from -3 to 3
- value_weight: bfloat16 [768, 768], P(None, 'head'), may hold values from -0.21875 to 0.21875
- out_weight: bfloat16 [768, 768], replicated, may hold values from -0.875 to 0.875
- norm2_gain: float32 [768], replicated, may hold values from 0.25 to 1.75
- norm2_bias: float32 [768], replicated, may hold values from -1.75 to 1.75
- up_weight: bfloat16 [768, 3072], P(None, 'head'), may hold values from -0.21875 to 0.21875
- up_bias: float32 [3072], P('head'), may hold values from -3 to 3
- down_weight: bfloat16 [3072, 768], P('head'), may hold values from -0.109375 to 0.109375
- down_bias: float32 [768], replicated, may hold values from -1.75 to 1.75
- out_grad: bfloat16 [16384, 768], P(('dp', 'head')), may hold values from -6 to 6
Outputs:
- result: float32 [16384, 768], P(('dp', 'head'))
- input_grad: float32 [16384, 768], P(('dp', 'head'))
- norm1_gain_grad: float32 [768], replicated
- norm1_bias_grad: float32 [768], replicated
- f1_weight_grad: float32 [12, 768, 768], P('head', 'dp')
- f1_bias_grad: float32 [12, 768], replicated
- f2_weight_grad: float32 [12, 768, 512], P('head', 'dp')
- f2_bias_grad: float32 [12, 512], replicated
- value_weight_grad: float32 [768, 768], P('dp', 'head')
- out_weight_grad: float32 [768, 768], P('dp')
- norm2_gain_grad: float32 [768], replicated
- norm2_bias_grad: float32 [768], replicated
- up_weight_grad: float32 [768, 3072], P('dp', 'head')
- up_bias_grad: float32 [3072], replicated
- down_weight_grad: float32 [3072, 768], P('head', 'dp')
- down_bias_grad: float32 [768], replicated
Inputs may be any that keep to these rules, and one draw needn't show every extreme that they name: `seq_len`: each aligned block of 512 rows is cut into sequences of 128, 256 or 512 rows, each starting at a multiple of its own length; every row of a sequence has its length.
All inputs are finite; a program needn't handle non-finite values.
Results may differ from a plain program's by a relative error of at most 0.017.
Values may be sent and summed in bfloat16 or wider, within the bound.
A program may use at most 256 MiB of HBM per device.

v0:
```python
import jax
import jax.numpy as jnp
from jax import lax
from jax.sharding import PartitionSpec as P


def normalize(values, gain, shift):
    centred = values - jnp.mean(values, -1, keepdims=True)
    inv_std = lax.rsqrt(jnp.mean(centred * centred, -1, keepdims=True) + 1e-05)
    scaled = centred * inv_std
    return (scaled, inv_std, scaled * gain + shift)


def norm_back(grad_out, scaled, inv_std, gain):
    grad_scaled = grad_out * gain
    centre_mean = jnp.mean(grad_scaled, -1, keepdims=True)
    cross_mean = jnp.mean(grad_scaled * scaled, -1, keepdims=True)
    return inv_std * (grad_scaled - centre_mean - scaled * cross_mean)


def silu_slope(pre_val):
    sigma = jax.nn.sigmoid(pre_val)
    return sigma * (1.0 + pre_val * (1.0 - sigma))


def spread_scores(scores, row_len, longest):
    half_len = longest // 2
    quarter_len = longest // 4
    twice = jnp.concatenate([scores[..., :half_len]] * 2, axis=-1)
    fourfold = jnp.concatenate([scores[..., :quarter_len]] * 4, axis=-1)
    return jnp.where(row_len == longest, scores, jnp.where(row_len == half_len, twice, fourfold))


def fold_scores(grads, row_len, longest):
    half_len = longest // 2
    quarter_len = longest // 4
    whole = jnp.where(row_len == longest, grads, 0.0)
    by_half = jnp.where(row_len == half_len, grads, 0.0)
    by_quarter = jnp.where(row_len == quarter_len, grads, 0.0)
    folded_half = by_half[..., :half_len] + by_half[..., half_len:]
    folded_quarter = (
        by_quarter[..., :quarter_len]
        + by_quarter[..., quarter_len:half_len]
        + by_quarter[..., half_len : half_len + quarter_len]
        + by_quarter[..., half_len + quarter_len :]
    )
    pad_half = jnp.zeros(folded_half.shape, jnp.float32)
    pad_quarter = jnp.zeros(folded_quarter.shape[:-1] + (longest - quarter_len,), jnp.float32)
    return (
        whole
        + jnp.concatenate([folded_half, pad_half], -1)
        + jnp.concatenate([folded_quarter, pad_quarter], -1)
    )


def masked_softmax(spread, seq_mask):
    floor_val = jnp.min(spread, -1, keepdims=True)
    top_val = jnp.max(jnp.where(seq_mask, spread, floor_val), -1, keepdims=True)
    exp_val = jnp.where(seq_mask, jnp.exp(spread - top_val), 0.0)
    return exp_val / jnp.sum(exp_val, -1, keepdims=True)


def local(
    tokens,
    seq_len,
    norm1_gain,
    norm1_bias,
    f1_weight,
    f1_bias,
    f2_weight,
    f2_bias,
    value_weight,
    out_weight,
    norm2_gain,
    norm2_bias,
    up_weight,
    up_bias,
    down_weight,
    down_bias,
    out_grad,
):
    own_rows = tokens.shape[0]
    model_width = tokens.shape[1]
    group_size = f2_weight.shape[0]
    longest = f2_weight.shape[2]
    head_dim = value_weight.shape[1] // group_size
    member_count = lax.axis_size("head")
    all_rows = own_rows * member_count
    slab_count = all_rows // longest
    quarter_len = longest // 4
    row_len = jnp.broadcast_to(seq_len[:, None], (seq_len.shape[0], quarter_len)).reshape(
        slab_count, longest, 1
    )
    positions = jnp.arange(longest, dtype=jnp.int32)
    seq_mask = positions[:, None] // row_len == positions[None, :] // row_len
    x_float = tokens.astype(jnp.float32)
    scaled_one, inv_one, normed_one = normalize(x_float, norm1_gain, norm1_bias)
    normed_one_low = normed_one.astype(jnp.bfloat16)
    gathered = lax.all_gather(normed_one_low, "head", axis=0, tiled=True)
    pre_one = (
        jnp.einsum("rd,hde->hre", gathered, f1_weight, preferred_element_type=jnp.float32)
        + f1_bias[:, None, :]
    )
    hidden = jax.nn.silu(pre_one).astype(jnp.bfloat16)
    scores = (
        jnp.einsum("hre,hel->hrl", hidden, f2_weight, preferred_element_type=jnp.float32)
        + f2_bias[:, None, :]
    )
    values = jnp.dot(gathered, value_weight, preferred_element_type=jnp.float32).astype(
        jnp.bfloat16
    )
    values_four = values.reshape(slab_count, longest, group_size, head_dim)
    spread = spread_scores(
        scores.reshape(group_size, slab_count, longest, longest), row_len, longest
    )
    probs = masked_softmax(spread, seq_mask)
    probs_low = probs.astype(jnp.bfloat16)
    mixed = jnp.einsum(
        "hnqk,nkhd->nqhd", probs_low, values_four, preferred_element_type=jnp.float32
    )
    mixed_low = mixed.reshape(all_rows, group_size * head_dim).astype(jnp.bfloat16)
    attended = lax.all_to_all(mixed_low, "head", split_axis=0, concat_axis=1, tiled=True)
    residual = x_float + jnp.dot(attended, out_weight, preferred_element_type=jnp.float32)
    scaled_two, inv_two, normed_two = normalize(residual, norm2_gain, norm2_bias)
    normed_two_low = normed_two.astype(jnp.bfloat16)
    gathered_mid = lax.all_gather(normed_two_low, "head", axis=0, tiled=True)
    pre_up = jnp.dot(gathered_mid, up_weight, preferred_element_type=jnp.float32) + up_bias
    act_low = jax.nn.silu(pre_up).astype(jnp.bfloat16)
    ffn_out = lax.psum_scatter(
        jnp.dot(act_low, down_weight, preferred_element_type=jnp.float32).astype(jnp.bfloat16),
        "head",
        scatter_dimension=0,
        tiled=True,
    ).astype(jnp.float32)
    result = residual + ffn_out + down_bias
    grad_float = out_grad.astype(jnp.float32)
    down_bias_grad = jnp.sum(grad_float, 0)
    grad_all = lax.all_gather(out_grad, "head", axis=0, tiled=True)
    down_grad = jnp.einsum("rf,rd->fd", act_low, grad_all, preferred_element_type=jnp.float32)
    act_grad = jnp.einsum("rd,fd->rf", grad_all, down_weight, preferred_element_type=jnp.float32)
    pre_up_grad = (act_grad * silu_slope(pre_up)).astype(jnp.bfloat16)
    up_bias_grad = jnp.sum(pre_up_grad.astype(jnp.float32), 0)
    up_grad = jnp.einsum("rd,rf->df", gathered_mid, pre_up_grad, preferred_element_type=jnp.float32)
    normed_two_grad = lax.psum_scatter(
        jnp.einsum("rf,df->rd", pre_up_grad, up_weight, preferred_element_type=jnp.float32).astype(
            jnp.bfloat16
        ),
        "head",
        scatter_dimension=0,
        tiled=True,
    ).astype(jnp.float32)
    norm2_gain_grad = jnp.sum(normed_two_grad * scaled_two, 0)
    norm2_bias_grad = jnp.sum(normed_two_grad, 0)
    residual_grad = grad_float + norm_back(normed_two_grad, scaled_two, inv_two, norm2_gain)
    residual_low = residual_grad.astype(jnp.bfloat16)
    out_grad_local = jnp.einsum(
        "rd,re->de", attended, residual_low, preferred_element_type=jnp.float32
    )
    attended_grad = jnp.einsum(
        "re,de->rd", residual_low, out_weight, preferred_element_type=jnp.float32
    ).astype(jnp.bfloat16)
    mixed_grad = lax.all_to_all(attended_grad, "head", split_axis=1, concat_axis=0, tiled=True)
    mixed_four = mixed_grad.reshape(slab_count, longest, group_size, head_dim)
    values_grad = jnp.einsum(
        "hnqk,nqhd->nkhd", probs_low, mixed_four, preferred_element_type=jnp.float32
    )
    values_grad = values_grad.reshape(all_rows, group_size * head_dim).astype(jnp.bfloat16)
    probs_grad = jnp.einsum(
        "nqhd,nkhd->hnqk", mixed_four, values_four, preferred_element_type=jnp.float32
    )
    spread_grad = probs * (probs_grad - jnp.sum(probs * probs_grad, -1, keepdims=True))
    scores_grad = (
        fold_scores(spread_grad, row_len, longest)
        .reshape(group_size, all_rows, longest)
        .astype(jnp.bfloat16)
    )
    f2_bias_grad = jnp.sum(scores_grad.astype(jnp.float32), 1)
    f2_grad = jnp.einsum("hre,hrl->hel", hidden, scores_grad, preferred_element_type=jnp.float32)
    hidden_grad = jnp.einsum(
        "hrl,hel->hre", scores_grad, f2_weight, preferred_element_type=jnp.float32
    )
    pre_one_grad = (hidden_grad * silu_slope(pre_one)).astype(jnp.bfloat16)
    f1_bias_grad = jnp.sum(pre_one_grad.astype(jnp.float32), 1)
    f1_grad = jnp.einsum("rd,hre->hde", gathered, pre_one_grad, preferred_element_type=jnp.float32)
    value_grad = jnp.einsum("rd,rc->dc", gathered, values_grad, preferred_element_type=jnp.float32)
    first_term = jnp.einsum(
        "hre,hde->rd", pre_one_grad, f1_weight, preferred_element_type=jnp.float32
    )
    normed_one_grad = lax.psum_scatter(
        (
            first_term
            + jnp.einsum("rc,dc->rd", values_grad, value_weight, preferred_element_type=jnp.float32)
        ).astype(jnp.bfloat16),
        "head",
        scatter_dimension=0,
        tiled=True,
    ).astype(jnp.float32)
    norm1_gain_grad = jnp.sum(normed_one_grad * scaled_one, 0)
    norm1_bias_grad = jnp.sum(normed_one_grad, 0)
    input_grad = residual_grad + norm_back(normed_one_grad, scaled_one, inv_one, norm1_gain)
    f1_piece, f2_piece, value_piece, out_piece, up_piece, down_piece = (
        lax.psum_scatter(f1_grad, "dp", scatter_dimension=1, tiled=True),
        lax.psum_scatter(f2_grad, "dp", scatter_dimension=1, tiled=True),
        lax.psum_scatter(value_grad, "dp", scatter_dimension=0, tiled=True),
        lax.psum_scatter(out_grad_local, "dp", scatter_dimension=0, tiled=True),
        lax.psum_scatter(up_grad, "dp", scatter_dimension=0, tiled=True),
        lax.psum_scatter(down_grad, "dp", scatter_dimension=1, tiled=True),
    )
    out_piece = lax.psum(out_piece.astype(jnp.bfloat16), "head").astype(jnp.float32)
    head_index = lax.axis_index("head")
    zero_index = jnp.int32(0)
    f1_bias_full = lax.dynamic_update_slice(
        jnp.zeros((group_size * member_count, model_width), jnp.float32),
        f1_bias_grad,
        (head_index * group_size, zero_index),
    )
    f2_bias_full = lax.dynamic_update_slice(
        jnp.zeros((group_size * member_count, longest), jnp.float32),
        f2_bias_grad,
        (head_index * group_size, zero_index),
    )
    ffn_width = up_bias.shape[0]
    up_bias_full = lax.dynamic_update_slice(
        jnp.zeros((ffn_width * member_count,), jnp.float32), up_bias_grad, (head_index * ffn_width,)
    )
    sums_out = lax.psum(
        (
            norm1_gain_grad,
            norm1_bias_grad,
            f1_bias_full,
            f2_bias_full,
            norm2_gain_grad,
            norm2_bias_grad,
            up_bias_full,
            down_bias_grad,
        ),
        ("dp", "head"),
    )
    return (
        result,
        input_grad,
        sums_out[0],
        sums_out[1],
        f1_piece,
        sums_out[2],
        f2_piece,
        sums_out[3],
        value_piece,
        out_piece,
        sums_out[4],
        sums_out[5],
        up_piece,
        sums_out[6],
        down_piece,
        sums_out[7],
    )


def solution(mesh):
    placed = (
        P(("dp", "head"), None),
        P("dp"),
        P(),
        P(),
        P("head", None, None),
        P("head", None),
        P("head", None, None),
        P("head", None),
        P(None, "head"),
        P(),
        P(),
        P(),
        P(None, "head"),
        P("head"),
        P("head", None),
        P(),
        P(("dp", "head"), None),
    )
    return jax.shard_map(
        local,
        mesh=mesh,
        in_specs=placed,
        out_specs=(
            P(("dp", "head"), None),
            P(("dp", "head"), None),
            P(),
            P(),
            P("head", "dp", None),
            P(),
            P("head", "dp", None),
            P(),
            P("dp", "head"),
            P("dp", None),
            P(),
            P(),
            P("dp", "head"),
            P(),
            P("head", "dp"),
            P(),
        ),
        check_vma=False,
    )
```

profile of v0, /device:TPU:0, one launch (start us, length us, event | category | flops | bytes accessed | tf_op | source)
XLA Modules:
  0.0 1146.8 jit_solution(749761618542051382)
XLA Ops:
  15.1 42.6 %fusion.25 = pred[2048,512]{1,0:T(8,128)(4,1)} fusion(s32[2048]{0:T(1024)S(1)} %bitcast.144, s32[512]{0:T(512)S(1)} %iota_sign_fusion, s32[2048]{0:T(1024)S(1)} %get-tuple-element.95, s32[2048]{0:T(1024)S(1)} %get-tuple-element.94), kind=kLoop, calls=%fused_computation.46 | loop fusion | flops 8388608 | bytes 1075200 | tf_op jit(solution)/shard_map/eq | solution.py:95
  57.7 42.4 %fusion.24 = pred[4,512,512]{2,1,0:T(8,128)(4,1)} fusion(s32[4,512]{1,0:T(4,128)S(1)} %bitcast.145, s32[4,512]{1,0:T(4,128)S(1)} %get-tuple-element.93, s32[512]{0:T(512)S(1)} %iota_sign_fusion, s32[4,512]{1,0:T(4,128)S(1)} %get-tuple-element.92), kind=kLoop, calls=%fused_computation.45 | loop fusion | flops 8388608 | bytes 1075200 | tf_op jit(solution)/shard_map/eq | solution.py:95
  100.2 15.9 %fusion.5 = (bf16[3,2048,768]{2,1,0:T(8,128)(2,1)}, f32[2048,3,768]{2,0,1:T(8,128)}) fusion(f32[3,768]{1,0:T(4,128)} %param.22, bf16[3,768,768]{2,1,0:T(8,128)(2,1)S(1)} %copy-done, bf16[2048,768]{1,0:T(8,128)(2,1)} %all-gather.4.cloned.1.call-done), kind=kOutput, calls=%fused_computation.8 | convolution fusion | flops 7276068864 | bytes 35005440 | tf_op jit(solution)/shard_map/rd,hde->hre/dot_general | solution.py:101
  116.1 7.6 broadcast_add_fusion
  137.4 12.0 %select_reduce_fusion.1 = f32[3,2048]{1,0:T(4,128)} fusion(f32[3,2048,512]{2,1,0:T(8,128)} %fusion.15, pred[2048,512]{1,0:T(8,128)(4,1)} %fusion.25), kind=kOutput, calls=%fused_computation.28 | output fusion | flops 6291967 | bytes 13656064 | tf_op jit(solution)/shard_map/jit(_where)/broadcast_in_dim | solution.py:58
  149.4 7.9 select_reduce_fusion
  167.2 17.5 %fusion.76 = (bf16[3,4,512,512]{3,2,1,0:T(8,128)(2,1)S(1)}, f32[3,4,512,512]{3,2,1,0:T(8,128)}) fusion(f32[3,4,512]{2,1,0:T(4,128)} %div.88, f32[3,4,512]{2,1,0:T(4,128)} %sub.89, f32[3,4,512,512]{3,2,1,0:T(8,128)} %bitcast.125, f32[3,4,512,128]{3,2,1,0:T(8,128)} %copy-done.3, f32[3,4,512,256]{3,2,1,0:T(8,128)} %copy-done.2, ...), kind=kLoop, calls=%fused_computation.136 | loop fusion | flops 31457280 | bytes 41996288 | tf_op jit(solution)/shard_map/convert_element_type | solution.py:117
  187.5 15.8 %all_to_all.32 = bf16[4,512,192]{1,2,0:T(8,128)(2,1)S(1)} all-to-all(bf16[4,512,192]{1,2,0:T(8,128)(2,1)S(1)} %bitcast.141), channel_id=1, replica_groups=mesh['dp'=8,'head'=4] {'head'}, dimensions={0} | all-to-all | bytes 1572864 | tf_op jit(solution)/shard_map/all_to_all | solution.py:122
  208.0 28.2 %all-gather.6.cloned.1.call-done = bf16[2048,768]{1,0:T(8,128)(2,1)} async-done(((bf16[512,768]{1,0:T(8,128)(2,1)}), bf16[2048,768]{1,0:T(8,128)(2,1)}) %all-gather.6.cloned.1.call-update) | async-done | bytes 3145744 | tf_op jit(solution)/shard_map/all_gather | solution.py:126
  236.2 9.1 multiply_convert_fusion.1
  245.3 21.0 %all-gather.8.cloned.1.call-done = bf16[2048,768]{1,0:T(8,128)(2,1)} async-done(((bf16[512,768]{1,0:T(8,128)(2,1)}), bf16[2048,768]{1,0:T(8,128)(2,1)}) %all-gather.8.cloned.1.call-update) | async-done | bytes 3145744 | tf_op jit(solution)/shard_map/all_gather | solution.py:138
  266.3 8.7 convert_reduce_fusion.2
  287.9 31.4 %reduce-scatter.14.cloned.1.call-done = bf16[512,768]{1,0:T(8,128)(2,1)} async-done(((bf16[2048,768]{1,0:T(8,128)(2,1)}), bf16[512,768]{1,0:T(8,128)(2,1)}) %reduce-scatter.14.cloned.1.call-update) | async-done | bytes 786448 | tf_op jit(solution)/shard_map/reduce_scatter | solution.py:144
  322.8 37.0 %reduce-scatter.12.cloned.1.call-done = bf16[512,768]{1,0:T(8,128)(2,1)} async-done(((bf16[2048,768]{1,0:T(8,128)(2,1)}), bf16[512,768]{1,0:T(8,128)(2,1)}) %reduce-scatter.12.cloned.1.call-update) | async-done | bytes 786448 | tf_op jit(solution)/shard_map/reduce_scatter | solution.py:129
  377.9 7.7 all-to-all-done.1
  390.0 7.6 fusion.66
  402.2 30.0 %broadcast_select_fusion.1 = (f32[3,4,512,512]{3,2,1,0:T(8,128)}, f32[3,4,512,512]{3,2,1,0:T(8,128)}, f32[3,4,512,512]{3,2,1,0:T(8,128)}) fusion(pred[4,512]{1,0:T(4,128)(4,1)S(1)} %get-tuple-element.91, pred[4,512]{1,0:T(4,128)(4,1)S(1)} %get-tuple-element.89, f32[3,4,512,512]{3,2,1,0:T(8,128)} %get-tuple-element.83, f32[3,4,512,512]{3,2,1,0:T(8,128)} %fusion.66), kind=kOutput, calls=%fused_computation.37 | output fusion | flops 15735295 | bytes 62918656 | tf_op jit(solution)/shard_map/sub | solution.py:171
  438.3 7.3 slice_add_fusion.1
  452.1 17.1 %convert_reduce_fusion = (f32[3,768]{1,0:T(4,128)}, bf16[3,2048,768]{2,1,0:T(8,128)(2,1)}) fusion(f32[2048,3,768]{2,0,1:T(8,128)} %get-tuple-element.100, f32[3,768]{1,0:T(4,128)S(1)} %copy-done.32, bf16[3,2048,512]{2,1,0:T(8,128)(2,1)} %bitcast.132, bf16[3,768,512]{2,1,0:T(8,128)(2,1)} %param.23), kind=kOutput, calls=%fused_computation.13 | convolution fusion | flops 4888459264 | bytes 36980736 | tf_op jit(solution)/shard_map/hrl,hel->hre/dot_general | solution.py:179
  469.2 13.4 %fusion.19 = bf16[2048,768]{1,0:T(8,128)(2,1)} fusion(f32[2048,768]{1,0:T(8,128)} %fusion.80, bf16[3,2048,768]{2,1,0:T(8,128)(2,1)} %get-tuple-element.107, bf16[3,768,768]{2,1,0:T(8,128)(2,1)S(1)} %copy-done), kind=kOutput, calls=%fused_computation.31 | convolution fusion | flops 7250903040 | bytes 22413312 | tf_op jit(solution)/shard_map/hre,hde->rd/dot_general | solution.py:186
  484.4 13.2 %fusion.32 = f32[3,768,768]{1,2,0:T(8,128)} fusion(bf16[3,2048,768]{2,1,0:T(8,128)(2,1)} %get-tuple-element.107, bf16[2048,768]{1,0:T(8,128)(2,1)} %all-gather.4.cloned.1.call-done), kind=kOutput, calls=%fused_computation.60 | convolution fusion | flops 7247757312 | bytes 19660800 | tf_op jit(solution)/shard_map/rd,hre->hde/dot_general | solution.py:184
  497.6 10.5 copy.63
  508.1 8.1 copy.70
  516.3 6.9 fusion.83
  523.4 7.0 fusion.84
  542.6 12.9 %fusion.81 = f32[3,768,512]{2,1,0:T(8,128)} fusion(bf16[3,2048,768]{2,1,0:T(8,128)(2,1)} %get-tuple-element.99, bf16[3,2048,512]{2,1,0:T(8,128)(2,1)} %bitcast.133), kind=kOutput, calls=%fused_computation.140 | convolution fusion | flops 4831838208 | bytes 20447232 | tf_op jit(solution)/shard_map/hre,hrl->hel/dot_general | solution.py:178
  561.5 126.3 %reduce-scatter.28.cloned.1.call-done = f32[96,2304]{1,0:T(8,128)} async-done(((f32[768,2304]{1,0:T(8,128)}), f32[96,2304]{1,0:T(8,128)}) %reduce-scatter.28.cloned.1.call-update) | async-done | bytes 884752
  692.6 67.8 %reduce-scatter.24.cloned.1.call-done = f32[96,768]{1,0:T(8,128)} async-done(((f32[768,768]{1,0:T(8,128)}), f32[96,768]{1,0:T(8,128)}) %reduce-scatter.24.cloned.1.call-update) | async-done | bytes 294928 | tf_op jit(solution)/shard_map/reduce_scatter | solution.py:206
  760.4 72.8 %reduce-scatter.26.cloned.1.call-done = f32[768,96]{0,1:T(8,128)} async-done(((f32[768,768]{0,1:T(8,128)}), f32[768,96]{0,1:T(8,128)}) %reduce-scatter.26.cloned.1.call-update) | async-done | bytes 294928 | tf_op jit(solution)/shard_map/reduce_scatter | solution.py:207
  833.2 65.6 %reduce-scatter.20.cloned.1.call-done = f32[96,192]{1,0:T(8,128)} async-done(((f32[768,192]{1,0:T(8,128)}), f32[96,192]{1,0:T(8,128)}) %reduce-scatter.20.cloned.1.call-update) | async-done | bytes 73744 | tf_op jit(solution)/shard_map/reduce_scatter | solution.py:204
  898.8 130.3 %all-reduce.8.cloned.1.call-done = (f32[768]{0:T(1024)}, f32[768]{0:T(1024)}, f32[12,768]{1,0:T(8,128)}, f32[12,512]{1,0:T(8,128)}, f32[768]{0:T(1024)}, /*index=5*/f32[768]{0:T(1024)}, f32[3072]{0:T(1024)}, f32[768]{0:T(1024)}) async-done(((f32[768]{0:T(1024)}, f32[768]{0:T(1024)}, f32[12,768]{1,0:T(8,128)}, f32[12,512]{1,0:T(8,128)}, f32[768]{0:T(1024)}, /*index=5*/f32[768]{0:T(1024)}, f32[3072]{0:T(1024)}, ...) | async-done | bytes 89104 | tf_op jit(solution)/shard_map/psum | solution.py:226
  1029.1 100.3 %reduce-scatter.18.cloned.1.call-done = f32[3,96,512]{2,1,0:T(8,128)} async-done(((f32[3,768,512]{2,1,0:T(8,128)}), f32[3,96,512]{2,1,0:T(8,128)}) %reduce-scatter.18.cloned.1.call-update) | async-done | bytes 589840 | tf_op jit(solution)/shard_map/reduce_scatter | solution.py:203
  (177 shorter events, 129.9 us)
Async XLA Ops:
  7.2 93.0 %copy-start = (bf16[3,768,768]{2,1,0:T(8,128)(2,1)S(1)}, bf16[3,768,768]{2,1,0:T(8,128)(2,1)}, u32[]{:S(2)}) copy-start(bf16[3,768,768]{2,1,0:T(8,128)(2,1)} %param.21) | copy-start | bytes 10616836
  7.2 92.9 %all-gather.4.cloned.1.call-start = ((), (), s32[]{:S(2)}) async-start(), calls=%async_computation.11 | async-start | bytes 3932160 | tf_op jit(solution)/shard_map/all_gather | solution.py:99
  13.2 223.0 %all-gather.6.cloned.1.call-start = ((), (), s32[]{:S(2)}) async-start(), calls=%async_computation.12 | async-start | bytes 3932160 | tf_op jit(solution)/shard_map/all_gather | solution.py:126
  100.1 15.9 %copy-start.33 = (f32[3,512]{1,0:T(4,128)S(1)}, f32[3,512]{1,0:T(4,128)}, u32[]{:S(2)}) copy-start(f32[3,512]{1,0:T(4,128)} %param.24) | copy-start | bytes 18436
  100.2 15.9 %copy-start.28 = (bf16[3,768,512]{2,1,0:T(8,128)(2,1)S(1)}, bf16[3,768,512]{2,1,0:T(8,128)(2,1)}, u32[]{:S(2)}) copy-start(bf16[3,768,512]{2,1,0:T(8,128)(2,1)} %param.23) | copy-start | bytes 7077892
  124.1 6.9 copy-start.24
  158.7 8.6 copy-start.21
  167.2 17.5 %copy-start.9 = (bf16[4,512,3,64]{1,0,3,2:T(4,128)(2,1)S(1)}, bf16[4,512,3,64]{1,0,3,2:T(4,128)(2,1)}, u32[]{:S(2)}) copy-start(bf16[4,512,3,64]{1,0,3,2:T(4,128)(2,1)} %reshape.271) | copy-start | bytes 2359300
  184.7 18.6 %copy-start.5 = (bf16[512,768]{1,0:T(8,128)(2,1)S(1)}, bf16[512,768]{1,0:T(8,128)(2,1)}, u32[]{:S(2)}) copy-start(bf16[512,768]{1,0:T(8,128)(2,1)} %param.17) | copy-start | bytes 2359300
  184.7 18.6 %copy-start.30 = (bf16[768,768]{1,0:T(8,128)(2,1)S(1)}, bf16[768,768]{1,0:T(8,128)(2,1)}, u32[]{:S(2)}) copy-start(bf16[768,768]{1,0:T(8,128)(2,1)} %param.26) | copy-start | bytes 3538948
  187.5 18.4 %copy-start.16 = (f32[768]{0:T(1024)S(1)}, f32[768]{0:T(1024)}, u32[]{:S(2)}) copy-start(f32[768]{0:T(1024)} %param.27) | copy-start | bytes 9220
  187.5 18.4 %copy-start.26 = (f32[768]{0:T(1024)S(1)}, f32[768]{0:T(1024)}, u32[]{:S(2)}) copy-start(f32[768]{0:T(1024)} %param.28) | copy-start | bytes 9220
  207.2 59.1 %all-gather.8.cloned.1.call-start = ((), (), s32[]{:S(2)}) async-start(), calls=%async_computation.14 | async-start | bytes 3932160 | tf_op jit(solution)/shard_map/all_gather | solution.py:138
  207.9 111.3 %reduce-scatter.14.cloned.1.call-start = ((), (), s32[]{:S(2)}) async-start(), calls=%async_computation.15 | async-start | bytes 3932160 | tf_op jit(solution)/shard_map/reduce_scatter | solution.py:144
  266.3 10.4 copy-start.29
  281.2 78.7 %reduce-scatter.12.cloned.1.call-start = ((), (), s32[]{:S(2)}) async-start(), calls=%async_computation.13 | async-start | bytes 3932160 | tf_op jit(solution)/shard_map/reduce_scatter | solution.py:129
  369.6 15.9 %all-to-all-start.1 = ((bf16[512,4,192]{0,2,1:T(8,128)(2,1)}), bf16[512,4,192]{0,2,1:T(8,128)(2,1)}, u32[]{:S(2)}, u32[]{:S(2)}) async-start(bf16[512,4,192]{0,2,1:T(8,128)(2,1)} %bitcast.139), calls=%async_computation.3 | async-start | bytes 1572864 | tf_op jit(solution)/shard_map/all_to_all | solution.py:162
  373.9 108.8 %reduce-scatter.22.cloned.1.call-start = ((), (), s32[]{:S(2)}) async-start(), calls=%async_computation.19 | async-start | bytes 2654208 | tf_op jit(solution)/shard_map/reduce_scatter | solution.py:205
  377.8 161.9 %reduce-scatter.16.cloned.1.call-start = ((), (), s32[]{:S(2)}) async-start(), calls=%async_computation.16 | async-start | bytes 3932160 | tf_op jit(solution)/shard_map/reduce_scatter | solution.py:189
  390.0 8.4 copy-start.12
  432.3 13.4 %slice-start = ((s8[12582912]{0:T(1024)(128)(4,1)}), s8[4194304]{0:T(1024)(128)(4,1)S(1)}, s32[]{:S(2)}) async-start(s8[12582912]{0:T(1024)(128)(4,1)} %bitcast.127), calls=%async_computation.25 | async-start | bytes 8388608
  432.3 13.4 %slice-start.1 = ((s8[12582912]{0:T(1024)(128)(4,1)}), s8[4194304]{0:T(1024)(128)(4,1)S(1)}, s32[]{:S(2)}) async-start(s8[12582912]{0:T(1024)(128)(4,1)} %bitcast.127), calls=%async_computation.26 | async-start | bytes 8388608
  438.3 7.3 slice-start.2
  438.3 7.3 copy-start.22
  482.6 72.9 %all-reduce.6.cloned.1.call-start = ((), (), s32[]{:S(2)}) async-start(), calls=%async_computation.20 | async-start | bytes 294912 | tf_op jit(solution)/shard_map/psum | solution.py:209
  484.3 203.5 %reduce-scatter.28.cloned.1.call-start = ((), (), s32[]{:S(2)}) async-start(), calls=%async_computation.23 | async-start | bytes 7962624
  516.3 244.2 %reduce-scatter.24.cloned.1.call-start = ((), (), s32[]{:S(2)}) async-start(), calls=%async_computation.21 | async-start | bytes 2654208 | tf_op jit(solution)/shard_map/reduce_scatter | solution.py:206
  523.3 309.9 %reduce-scatter.26.cloned.1.call-start = ((), (), s32[]{:S(2)}) async-start(), calls=%async_computation.22 | async-start | bytes 2654208 | tf_op jit(solution)/shard_map/reduce_scatter | solution.py:207
  530.4 9.4 copy-start.14
  530.4 368.4 %reduce-scatter.20.cloned.1.call-start = ((), (), s32[]{:S(2)}) async-start(), calls=%async_computation.18 | async-start | bytes 884736 | tf_op jit(solution)/shard_map/reduce_scatter | solution.py:204
  534.7 494.4 %all-reduce.8.cloned.1.call-start = ((), (), s32[]{:S(2)}) async-start(), calls=%async_computation.24 | async-start | bytes 229376 | tf_op jit(solution)/shard_map/psum | solution.py:226
  542.6 586.8 %reduce-scatter.18.cloned.1.call-start = ((), (), s32[]{:S(2)}) async-start(), calls=%async_computation.17 | async-start | bytes 5308416 | tf_op jit(solution)/shard_map/reduce_scatter | solution.py:203
  (21 other events, 73.5 us)
Sparse Core Ops, SparseCore 0:
  13.4 31.2 all-gather.3
  207.3 28.8 all-gather.5
  237.8 28.5 all-gather.7
  281.3 37.9 reduce-scatter.13
  321.8 37.9 reduce-scatter.11
  377.9 70.3 reduce-scatter.21
  482.7 37.7 reduce-scatter.15
  523.5 30.7 all-reduce.5
  558.0 129.7 reduce-scatter.27
  692.1 68.2 reduce-scatter.23
  764.9 68.2 reduce-scatter.25
  837.3 61.4 reduce-scatter.19
  906.4 122.6 all-reduce.7
  1033.1 96.1 reduce-scatter.17
where the time goes:
time: 1160 us; the launch traced here: 1150 us
  waiting for transfers between devices  689 us (59%)
  other arithmetic  205 us (18%)
  matrix products  155 us (13%)
  local copies, waits for them, and re-layouts  61.1 us (5%)
  blocking collectives  15.8 us (1%)
  between operations  14.8 us (1%)
    psum x1, waiting for transfers between devices, local(): lax.psum((norm1_gain_grad, norm1_bias_grad, f1_bias_full, f2_bias_full, n...  130 us
    unnamed x15, waiting for transfers between devices  127 us
    reduce_scatter x1, waiting for transfers between devices, local(): lax.psum_scatter(f2_grad, 'dp', scatter_dimension=1, tiled=True)  100 us
    eq x2, other arithmetic, local(): seq_mask = positions[:, None] // row_len == positions[None, :] // row_len  85.1 us
    reduce_scatter x1, waiting for transfers between devices, local(): lax.psum_scatter(down_grad, 'dp', scatter_dimension=1, tiled=True)  72.8 us
    reduce_scatter x1, waiting for transfers between devices, local(): lax.psum_scatter(up_grad, 'dp', scatter_dimension=0, tiled=True)  67.8 us
    reduce_scatter x1, waiting for transfers between devices, local(): lax.psum_scatter(value_grad, 'dp', scatter_dimension=0, tiled=True)  65.6 us
    unnamed x94, local copies, waits for them, and re-layouts  45.9 us
  transfers between devices with their start and end apart: 15, of which 11 were waited for; matrix products, arithmetic and copies ran while one was open for 25% of the time, Pallas kernels for 0%

commit v1 on v0

v1 whole, which is shorter than its diff:
```python
import functools

import jax
import jax.numpy as jnp
from jax import lax
from jax.experimental import pallas as pl
from jax.experimental.pallas import tpu as pltpu
from jax.sharding import PartitionSpec as P

F32 = jnp.float32
BF16 = jnp.bfloat16
BLOCK = 128
VMEM_LIMIT = 50 << 20


def mm(a, b):
    return lax.dot_general(a, b, (((1,), (0,)), ((), ())), preferred_element_type=F32)


def mm_nt(a, b):
    return lax.dot_general(a, b, (((1,), (1,)), ((), ())), preferred_element_type=F32)


def mm_tn(a, b):
    return lax.dot_general(a, b, (((0,), (0,)), ((), ())), preferred_element_type=F32)


def standardize(values):
    centred = values - jnp.mean(values, -1, keepdims=True)
    inv_std = lax.rsqrt(jnp.mean(centred * centred, -1, keepdims=True) + 1e-05)
    return centred * inv_std, inv_std


def norm_back(grad_out, scaled, inv_std, gain):
    grad_scaled = grad_out * gain
    centre_mean = jnp.mean(grad_scaled, -1, keepdims=True)
    cross_mean = jnp.mean(grad_scaled * scaled, -1, keepdims=True)
    return inv_std * (grad_scaled - centre_mean - scaled * cross_mean)


def silu_and_slope(pre_val):
    sigma = 0.5 + 0.5 * jnp.tanh(0.5 * pre_val)
    gated = pre_val * sigma
    return gated, sigma + gated * (1.0 - sigma)


def swap(value, axis, step):
    return lax.ppermute(value, axis, [(i, i ^ step) for i in range(lax.axis_size(axis))])


def whole(shape):
    return pl.BlockSpec(shape, lambda *_: (0,) * len(shape))


def params(steps=1):
    return pltpu.CompilerParams(
        dimension_semantics=("arbitrary",) * steps, vmem_limit_bytes=VMEM_LIMIT
    )


def cost(macs, bytes_accessed):
    return pl.CostEstimate(flops=2 * macs, bytes_accessed=bytes_accessed, transcendentals=0)


def head_forward_kernel(
    step,
    lens_ref,
    x_ref,
    gain_ref,
    bias_ref,
    f1_ref,
    f1b_ref,
    f2_ref,
    f2b_ref,
    vt_ref,
    *rest,
):
    n1_ref, n1t_ref, hid_ref, slope_ref, prob_ref, valt_ref, mixt_ref = rest[-7:]
    rows, longest = prob_ref.shape[-2:]
    blocks = longest // BLOCK

    @pl.when(pl.program_id(0) == 0)
    def _():
        scaled, _ = standardize(x_ref[...].astype(F32))
        low = (scaled * gain_ref[...] + bias_ref[...]).astype(BF16)
        n1_ref[...] = low
        n1t_ref[0] = low.T

    valt = mm(vt_ref[0], n1t_ref[0]).astype(BF16)
    valt_ref[0, 0] = valt
    pre = mm(n1_ref[...], f1_ref[0]) + f1b_ref[0]
    gated, slope = silu_and_slope(pre)
    hidden = gated.astype(BF16)
    hid_ref[0, 0] = hidden
    slope_ref[0, 0] = slope.astype(BF16)
    scores = mm(hidden, f2_ref[0]) + f2b_ref[0]
    first = jnp.bitwise_xor(lax.axis_index("head"), step) * blocks
    column = lax.broadcasted_iota(jnp.int32, (BLOCK, longest), 1)
    for b in range(rows // BLOCK):
        length = lens_ref[first + b]
        own = scores[b * BLOCK : (b + 1) * BLOCK]
        keep = column < length
        top = jnp.max(jnp.where(keep, own, -3.0e38), -1, keepdims=True)
        exp_val = jnp.where(keep, jnp.exp(own - top), 0.0)
        prob = exp_val * (1.0 / jnp.sum(exp_val, -1, keepdims=True))
        parts = [prob[:, c * BLOCK : (c + 1) * BLOCK] for c in range(blocks)]
        zero = jnp.zeros((BLOCK, BLOCK), F32)
        is_full = length == longest
        is_half = length == longest // 2
        for c in range(blocks):
            half = parts[c % 2] if c // 2 == b // 2 else zero
            quarter = parts[0] if c == b else zero
            cell = jnp.where(is_full, parts[c], jnp.where(is_half, half, quarter))
            prob_ref[0, 0, b * BLOCK : (b + 1) * BLOCK, c * BLOCK : (c + 1) * BLOCK] = cell.astype(
                BF16
            )
    mixt_ref[...] = mm_nt(valt, prob_ref[0, 0]).astype(BF16)


def head_forward(step, kept, seq_len, x, gain, bias, f1, f1b, f2, f2b, vt):
    heads, width, longest = f2.shape
    rows = x.shape[0]
    dim = vt.shape[1]
    slabs = lax.axis_size("head")
    stacked = [
        ((slabs, width, rows), (1, width, rows), lambda h: (step, 0, 0)),
        ((slabs, heads, rows, width), (1, 1, rows, width), lambda h: (step, h, 0, 0)),
        ((slabs, heads, rows, width), (1, 1, rows, width), lambda h: (step, h, 0, 0)),
        ((slabs, heads, rows, longest), (1, 1, rows, longest), lambda h: (step, h, 0, 0)),
        ((slabs, heads, dim, rows), (1, 1, dim, rows), lambda h: (step, h, 0, 0)),
    ]
    out_shape = (
        [jax.ShapeDtypeStruct((rows, width), BF16)]
        + [jax.ShapeDtypeStruct(shape, BF16) for shape, _, _ in stacked]
        + [jax.ShapeDtypeStruct((heads * dim, rows), BF16)]
    )
    out_specs = (
        [whole((rows, width))]
        + [pl.BlockSpec(block, index) for _, block, index in stacked]
        + [pl.BlockSpec((dim, rows), lambda h: (h, 0))]
    )
    in_specs = [
        pl.BlockSpec(memory_space=pltpu.SMEM),
        whole((rows, width)),
        whole((1, width)),
        whole((1, width)),
        pl.BlockSpec((1, width, width), lambda h: (h, 0, 0)),
        pl.BlockSpec((1, 1, width), lambda h: (h, 0, 0)),
        pl.BlockSpec((1, width, longest), lambda h: (h, 0, 0)),
        pl.BlockSpec((1, 1, longest), lambda h: (h, 0, 0)),
        pl.BlockSpec((1, dim, width), lambda h: (h, 0, 0)),
    ]
    args = [seq_len, x, gain, bias, f1, f1b, f2, f2b, vt]
    aliases = {}
    if kept is not None:
        for i, buffer in enumerate(kept):
            aliases[len(args)] = 1 + i
            args.append(buffer)
            in_specs.append(pl.BlockSpec(memory_space=pl.ANY))
    outs = pl.pallas_call(
        functools.partial(head_forward_kernel, step),
        grid=(heads,),
        out_shape=out_shape,
        in_specs=in_specs,
        out_specs=out_specs,
        input_output_aliases=aliases,
        compiler_params=params(),
        cost_estimate=cost(heads * rows * width * (width + longest + 128), 14 << 20),
        name="head_forward",
    )(*args)
    return outs[1:6], outs[6]


def residual_kernel(*refs):
    pieces = refs[:-7]
    x_ref, ow_ref, gain_ref, bias_ref, res_ref, n2_ref, attt_ref = refs[-7:]
    depth = pieces[0].shape[0]
    me = lax.axis_index("head")
    for j, piece in enumerate(pieces):
        start = pl.multiple_of(jnp.bitwise_xor(me, j) * depth, depth)
        attt_ref[pl.ds(start, depth), :] = piece[...]
    residual = x_ref[...].astype(F32) + mm_tn(attt_ref[...], ow_ref[...])
    res_ref[...] = residual
    scaled, _ = standardize(residual)
    n2_ref[...] = (scaled * gain_ref[...] + bias_ref[...]).astype(BF16)


def residual_and_norm(pieces, x, ow, gain, bias):
    rows, width = x.shape
    return pl.pallas_call(
        residual_kernel,
        out_shape=[
            jax.ShapeDtypeStruct((rows, width), F32),
            jax.ShapeDtypeStruct((rows, width), BF16),
            jax.ShapeDtypeStruct((width, rows), BF16),
        ],
        compiler_params=pltpu.CompilerParams(vmem_limit_bytes=VMEM_LIMIT),
        cost_estimate=cost(rows * width * width, 7 << 20),
        name="residual_and_norm",
    )(*pieces, x, ow, gain, bias)


def ffn_kernel(n2_ref, og_ref, up_ref, upb_ref, down_ref, n2g_ref, ffn_ref, act_ref, pug_ref):
    pre = mm(n2_ref[...], up_ref[...]) + upb_ref[...]
    gated, slope = silu_and_slope(pre)
    act = gated.astype(BF16)
    act_ref[...] = act
    pug = (mm_nt(og_ref[...], down_ref[...]) * slope).astype(BF16)
    pug_ref[...] = pug
    n2g_ref[...] = mm_nt(pug, up_ref[...]).astype(BF16)
    ffn_ref[...] = mm(act, down_ref[...]).astype(BF16)


def ffn(n2, og, up, upb, down):
    rows, width = n2.shape
    units = up.shape[1]
    shapes = [(rows, width), (rows, width), (rows, units), (rows, units)]
    return pl.pallas_call(
        ffn_kernel,
        out_shape=[jax.ShapeDtypeStruct(s, BF16) for s in shapes],
        compiler_params=pltpu.CompilerParams(vmem_limit_bytes=VMEM_LIMIT),
        cost_estimate=cost(4 * rows * width * units, 7 << 20),
        name="ffn",
    )(n2, og, up, upb, down)


def store_shards(keep_ref, send_ref, lanes, acc_ref):
    count, depth = keep_ref.shape[:2]
    me = lax.axis_index("dp")
    pair, parity = me // 2, me % 2
    for k in range(count):
        other = jnp.bitwise_xor(pair, k) * 2
        mine = pl.multiple_of((other + parity) * depth, 8)
        theirs = pl.multiple_of((other + 1 - parity) * depth, 8)
        keep_ref[k, :, lanes] = acc_ref[pl.ds(mine, depth), :].astype(BF16)
        send_ref[k, :, lanes] = acc_ref[pl.ds(theirs, depth), :].astype(BF16)


def shard_shape(width, lanes):
    members = lax.axis_size("dp")
    return jax.ShapeDtypeStruct((members // 2, width // members, lanes), BF16)


def ffn_grads_kernel(slabs, *refs):
    og, n2, act, pug = (refs[i * slabs : (i + 1) * slabs] for i in range(4))
    keep_ref, send_ref, upb_ref, down_acc, up_acc = refs[4 * slabs :]
    step = pl.program_id(0)
    tile = og[0].shape[1]
    units = act[0].shape[1]
    rows = pl.ds(pl.multiple_of(step * tile, tile), tile)
    down_acc[rows, :] = sum(mm_tn(og[j][...], act[j][...]) for j in range(slabs))
    up_acc[rows, :] = sum(mm_tn(n2[j][...], pug[j][...]) for j in range(slabs))

    @pl.when(step == pl.num_programs(0) - 1)
    def _():
        upb_ref[...] = sum(
            jnp.sum(pug[j][...].astype(F32), 0, keepdims=True) for j in range(slabs)
        )
        store_shards(keep_ref, send_ref, slice(0, units), down_acc)
        store_shards(keep_ref, send_ref, slice(units, 2 * units), up_acc)


def ffn_grads(og, n2, act, pug):
    slabs = len(og)
    rows, width = og[0].shape
    units = act[0].shape[1]
    tile = width // 2
    shards = shard_shape(width, 2 * units)
    left = pl.BlockSpec((rows, tile), lambda t: (0, t))
    return pl.pallas_call(
        functools.partial(ffn_grads_kernel, slabs),
        grid=(width // tile,),
        out_shape=[shards, shards, jax.ShapeDtypeStruct((1, units), F32)],
        in_specs=[left] * (2 * slabs) + [whole((rows, units))] * (2 * slabs),
        out_specs=[whole(shards.shape), whole(shards.shape), whole((1, units))],
        scratch_shapes=[pltpu.VMEM((width, units), F32)] * 2,
        compiler_params=params(),
        cost_estimate=cost(2 * slabs * rows * width * units, 18 << 20),
        name="ffn_grads",
    )(*og, *n2, *act, *pug)


def residual_back_kernel(
    t0_ref, t1_ref, t2_ref, res_ref, og_ref, gain_ref, ow_ref, *outs
):
    rg_ref, rl_ref, sums_ref, mgt_ref = outs[0], outs[1], outs[2], outs[-1]
    pieces = outs[3:-1]
    grad = t0_ref[...].astype(F32) + t1_ref[...].astype(F32) + t2_ref[...].astype(F32)
    scaled, inv_std = standardize(res_ref[...])
    cot = og_ref[...].astype(F32)
    res_grad = cot + norm_back(grad, scaled, inv_std, gain_ref[...])
    rg_ref[...] = res_grad
    low = res_grad.astype(BF16)
    rl_ref[...] = low
    sums_ref[0:1, :] = jnp.sum(grad * scaled, 0, keepdims=True)
    sums_ref[1:2, :] = jnp.sum(grad, 0, keepdims=True)
    sums_ref[2:3, :] = jnp.sum(cot, 0, keepdims=True)
    mgt_ref[...] = mm_nt(ow_ref[...], low).astype(BF16)
    depth = pieces[0].shape[0]
    me = lax.axis_index("head")
    for j, piece in enumerate(pieces):
        start = pl.multiple_of(jnp.bitwise_xor(me, j) * depth, depth)
        piece[...] = mgt_ref[pl.ds(start, depth), :]


def residual_back(terms, residual, og, gain, ow, members):
    rows, width = residual.shape
    piece = jax.ShapeDtypeStruct((width // members, rows), BF16)
    return pl.pallas_call(
        residual_back_kernel,
        out_shape=[
            jax.ShapeDtypeStruct((rows, width), F32),
            jax.ShapeDtypeStruct((rows, width), BF16),
            jax.ShapeDtypeStruct((3, width), F32),
        ]
        + [piece] * members,
        scratch_shapes=[pltpu.VMEM((width, rows), BF16)],
        compiler_params=pltpu.CompilerParams(vmem_limit_bytes=VMEM_LIMIT),
        cost_estimate=cost(rows * width * width, 9 << 20),
        name="residual_back",
    )(*terms, residual, og, gain, ow)


def out_grad_kernel(attt_ref, rl_ref, keep_ref, send_ref, acc_ref):
    acc_ref[...] = mm(attt_ref[...], rl_ref[...])
    store_shards(keep_ref, send_ref, slice(None), acc_ref)


def out_weight_grads(attt, low):
    width = attt.shape[0]
    shards = shard_shape(width, low.shape[1])
    return pl.pallas_call(
        out_grad_kernel,
        out_shape=[shards, shards],
        scratch_shapes=[pltpu.VMEM((width, low.shape[1]), F32)],
        compiler_params=pltpu.CompilerParams(vmem_limit_bytes=VMEM_LIMIT),
        cost_estimate=cost(attt.shape[1] * width * width, 3 << 20),
        name="out_weight_grads",
    )(attt, low)


def head_back_kernel(
    lens_ref,
    prob_ref,
    valt_ref,
    mgt_ref,
    hid_ref,
    slope_ref,
    n1t_ref,
    f2_ref,
    pog_ref,
    vgt_ref,
    f1b_ref,
    f2b_ref,
    keep_ref,
    send_ref,
    sg_ref,
    f1_acc,
    f2_acc,
    value_acc,
):
    j = pl.program_id(0)
    rows, longest = prob_ref.shape[-2:]
    blocks = longest // BLOCK

    @pl.when(j == 0)
    def _():
        f1_acc[...] = jnp.zeros_like(f1_acc)
        f2_acc[...] = jnp.zeros_like(f2_acc)
        value_acc[...] = jnp.zeros_like(value_acc)
        f1b_ref[...] = jnp.zeros_like(f1b_ref)
        f2b_ref[...] = jnp.zeros_like(f2b_ref)

    prob_low = prob_ref[0, 0]
    mgt = mgt_ref[0]
    vgt = mm(mgt, prob_low).astype(BF16)
    vgt_ref[0] = vgt
    probs_grad = mm_tn(mgt, valt_ref[0, 0])
    first = jnp.bitwise_xor(lax.axis_index("head"), j) * blocks
    for b in range(rows // BLOCK):
        length = lens_ref[first + b]
        own = slice(b * BLOCK, (b + 1) * BLOCK)
        prob = prob_low[own].astype(F32)
        grad = probs_grad[own]
        inner = jnp.sum(prob * grad, -1, keepdims=True)
        spread_grad = prob * (grad - inner)
        parts = [spread_grad[:, c * BLOCK : (c + 1) * BLOCK] for c in range(blocks)]
        zero = jnp.zeros((BLOCK, BLOCK), F32)
        is_full = length == longest
        is_half = length == longest // 2
        for c in range(blocks):
            half = parts[2 * (b // 2) + c] if c < 2 else zero
            quarter = parts[b] if c == 0 else zero
            cell = jnp.where(is_full, parts[c], jnp.where(is_half, half, quarter))
            sg_ref[own, c * BLOCK : (c + 1) * BLOCK] = cell.astype(BF16)
    scores_grad = sg_ref[...]
    f2b_ref[...] += jnp.sum(scores_grad.astype(F32), 0, keepdims=True)
    hidden_grad = mm_nt(scores_grad, f2_ref[0])
    pog = (hidden_grad * slope_ref[0, 0].astype(F32)).astype(BF16)
    pog_ref[0] = pog
    f1b_ref[...] += jnp.sum(pog.astype(F32), 0, keepdims=True)
    f2_acc[...] += mm_tn(hid_ref[0, 0], scores_grad)
    n1t = n1t_ref[0]
    f1_acc[...] += mm(n1t, pog)
    value_acc[...] += mm_nt(n1t, vgt)

    @pl.when(j == pl.num_programs(0) - 1)
    def _():
        width = f1_acc.shape[1]
        dim = value_acc.shape[1]
        store_shards(keep_ref, send_ref, slice(0, width), f1_acc)
        store_shards(keep_ref, send_ref, slice(width, width + longest), f2_acc)
        store_shards(
            keep_ref, send_ref, slice(width + longest, width + longest + dim), value_acc
        )


def head_back(h, seq_len, prob, valt, mgt, hid, slope, n1t, f2):
    slabs, heads, rows, longest = prob.shape
    width = hid.shape[3]
    dim = valt.shape[2]
    shards = shard_shape(width, width + longest + dim)
    by_head = lambda j: (j, h, 0, 0)
    by_slab = lambda j: (j, 0, 0)
    return pl.pallas_call(
        head_back_kernel,
        grid=(slabs,),
        out_shape=[
            jax.ShapeDtypeStruct((slabs, rows, width), BF16),
            jax.ShapeDtypeStruct((slabs, dim, rows), BF16),
            jax.ShapeDtypeStruct((1, width), F32),
            jax.ShapeDtypeStruct((1, longest), F32),
            shards,
            shards,
        ],
        in_specs=[
            pl.BlockSpec(memory_space=pltpu.SMEM),
            pl.BlockSpec((1, 1, rows, longest), by_head),
            pl.BlockSpec((1, 1, dim, rows), by_head),
            pl.BlockSpec((1, dim, rows), lambda j: (j, h, 0)),
            pl.BlockSpec((1, 1, rows, width), by_head),
            pl.BlockSpec((1, 1, rows, width), by_head),
            pl.BlockSpec((1, width, rows), by_slab),
            pl.BlockSpec((1, width, longest), lambda j: (h, 0, 0)),
        ],
        out_specs=[
            pl.BlockSpec((1, rows, width), by_slab),
            pl.BlockSpec((1, dim, rows), by_slab),
            whole((1, width)),
            whole((1, longest)),
            whole(shards.shape),
            whole(shards.shape),
        ],
        scratch_shapes=[
            pltpu.VMEM((rows, longest), BF16),
            pltpu.VMEM((width, width), F32),
            pltpu.VMEM((width, longest), F32),
            pltpu.VMEM((width, dim), F32),
        ],
        compiler_params=params(),
        cost_estimate=cost(slabs * rows * width * (width + 2 * longest + 256), 20 << 20),
        name="head_back",
    )(seq_len, prob, valt, mgt, hid, slope, n1t, f2)


def input_term_kernel(heads, *refs):
    pogs, vgts = refs[:heads], refs[heads : 2 * heads]
    f1_ref, vt_ref, x_ref, sums_in, out_ref, sums_ref = refs[2 * heads :]
    term = mm_nt(pogs[0][0], f1_ref[0])
    for h in range(1, heads):
        term += mm_nt(pogs[h][0], f1_ref[h])
    for h in range(heads):
        term += mm_tn(vgts[h][0], vt_ref[h])
    low = term.astype(BF16)
    out_ref[...] = low
    wide = low.astype(F32)
    scaled, _ = standardize(x_ref[...].astype(F32))
    sums_ref[0:1, :] = sums_in[0:1, :] + jnp.sum(wide * scaled, 0, keepdims=True)
    sums_ref[1:2, :] = sums_in[1:2, :] + jnp.sum(wide, 0, keepdims=True)


def input_term(j, pogs, vgts, f1, vt, x, sums):
    heads = len(pogs)
    slabs, rows, width = pogs[0].shape
    dim = vgts[0].shape[1]
    slab = lambda _: (j, 0, 0)
    return pl.pallas_call(
        functools.partial(input_term_kernel, heads),
        grid=(1,),
        out_shape=[
            jax.ShapeDtypeStruct((rows, width), BF16),
            jax.ShapeDtypeStruct((2, width), F32),
        ],
        in_specs=[pl.BlockSpec((1, rows, width), slab)] * heads
        + [pl.BlockSpec((1, dim, rows), slab)] * heads
        + [whole(f1.shape), whole(vt.shape), whole((rows, width)), whole((2, width))],
        out_specs=[whole((rows, width)), whole((2, width))],
        compiler_params=params(),
        cost_estimate=cost(heads * rows * width * (width + 256), 8 << 20),
        name="input_term",
    )(*pogs, *vgts, f1, vt, x, sums)


def input_back_kernel(t0_ref, t1_ref, t2_ref, x_ref, rg_ref, gain_ref, out_ref):
    grad = t0_ref[...].astype(F32) + t1_ref[...].astype(F32) + t2_ref[...].astype(F32)
    scaled, inv_std = standardize(x_ref[...].astype(F32))
    out_ref[...] = rg_ref[...] + norm_back(grad, scaled, inv_std, gain_ref[...])


def input_back(terms, x, res_grad, gain):
    return pl.pallas_call(
        input_back_kernel,
        out_shape=jax.ShapeDtypeStruct(res_grad.shape, F32),
        compiler_params=pltpu.CompilerParams(vmem_limit_bytes=VMEM_LIMIT),
        cost_estimate=cost(0, 7 << 20),
        name="input_back",
    )(*terms, x, res_grad, gain)


def gather_group(own):
    near = swap(own, "head", 1)
    far = swap(own, "head", 2)
    return [own, near, far, swap(far, "head", 1)]


def add_low(a, b):
    return (a.astype(F32) + b.astype(F32)).astype(BF16)


def scatter_terms(terms):
    cross = swap(add_low(terms[2], swap(terms[3], "head", 1)), "head", 2)
    return [terms[0], swap(terms[1], "head", 1), cross]


def reduce_over_dp(keep, send):
    both = keep.astype(F32) + swap(send, "dp", 1).astype(F32)
    total = both[0]
    low = both.astype(BF16)
    for k in range(1, keep.shape[0]):
        total = total + swap(low[k], "dp", 2 * k).astype(F32)
    return total


def local(
    tokens,
    seq_len,
    norm1_gain,
    norm1_bias,
    f1_weight,
    f1_bias,
    f2_weight,
    f2_bias,
    value_weight,
    out_weight,
    norm2_gain,
    norm2_bias,
    up_weight,
    up_bias,
    down_weight,
    down_bias,
    out_grad,
):
    members = lax.axis_size("head")
    heads, width, longest = f2_weight.shape
    units = up_weight.shape[1]
    dim = value_weight.shape[1] // heads
    row = lambda v: v.reshape(1, -1)
    vt = value_weight.T.reshape(heads, dim, width)
    f1b = f1_bias.reshape(heads, 1, width)
    f2b = f2_bias.reshape(heads, 1, longest)

    xs = gather_group(tokens)
    cot, _ = lax.optimization_barrier((out_grad, xs[2]))
    kept = None
    pieces = []
    for j in range(members):
        kept, mixt = head_forward(
            j,
            kept,
            seq_len,
            xs[j],
            row(norm1_gain),
            row(norm1_bias),
            f1_weight,
            f1b,
            f2_weight,
            f2b,
            vt,
        )
        pieces.append(mixt if j == 0 else swap(mixt, "head", j))
    n1t, hid, slope, prob, valt = kept
    residual, n2, attt = residual_and_norm(
        pieces, tokens, out_weight, row(norm2_gain), row(norm2_bias)
    )
    ogs = gather_group(cot)
    n2s = gather_group(n2)
    n2g, ffn_out, act, pug = zip(
        *[ffn(n2s[j], ogs[j], up_weight, row(up_bias), down_weight) for j in range(members)]
    )
    grad_terms = scatter_terms(n2g)
    ffn_keep, ffn_send, upb = ffn_grads(ogs, n2s, act, pug)
    res_grad, res_low, sums2, *mgts = residual_back(
        grad_terms, residual, out_grad, row(norm2_gain), out_weight, members
    )
    mgt = jnp.stack([m if j == 0 else swap(m, "head", j) for j, m in enumerate(mgts)])
    out_keep, out_send = out_weight_grads(attt, res_low)
    ffn_terms = scatter_terms(ffn_out)
    result = residual + sum(t.astype(F32) for t in ffn_terms) + down_bias

    backs = [
        head_back(h, seq_len, prob, valt, mgt, hid, slope, n1t, f2_weight) for h in range(heads)
    ]
    pogs, vgts, f1bg, f2bg, head_keep, head_send = zip(*backs)
    sums1 = jnp.zeros((2, width), F32)
    terms = [None] * members
    for j in reversed(range(members)):
        terms[j], sums1 = input_term(j, pogs, vgts, f1_weight, vt, xs[j], sums1)
    input_grad = input_back(scatter_terms(terms), tokens, res_grad, row(norm1_gain))

    ffn_total = reduce_over_dp(ffn_keep, ffn_send)
    out_total = reduce_over_dp(out_keep, out_send)
    head_totals = [reduce_over_dp(k, s) for k, s in zip(head_keep, head_send)]
    low = out_total.astype(BF16)
    low = add_low(low, swap(low, "head", 1))
    out_piece = low.astype(F32) + swap(low, "head", 2).astype(F32)

    own = jnp.concatenate(
        [v.reshape(-1) for v in f1bg] + [v.reshape(-1) for v in f2bg] + [upb.reshape(-1)]
    )
    shared = jnp.concatenate([sums1.reshape(-1), sums2.reshape(-1)])
    split = own.shape[0]
    vec = jnp.concatenate([own, shared]).reshape(-1, 128)
    step = 1
    while step < lax.axis_size("dp"):
        vec = vec + swap(vec, "dp", step)
        step *= 2
    flat = vec.reshape(-1)
    own, shared = flat[:split].reshape(1, -1), flat[split:]
    step = 1
    while step < members:
        got = swap(jnp.concatenate([own.reshape(-1), shared]).reshape(-1, 128), "head", step)
        got = got.reshape(-1)
        shared = shared + got[own.size :]
        own = jnp.concatenate([own, got[: own.size].reshape(own.shape)])
        step *= 2
    order = jnp.bitwise_xor(jnp.arange(members), lax.axis_index("head"))
    own = own[order]
    f1b_all = own[:, : heads * width].reshape(members * heads, width)
    f2b_all = own[:, heads * width : heads * (width + longest)].reshape(members * heads, longest)
    upb_all = own[:, heads * (width + longest) :].reshape(members * units)
    shared = shared.reshape(5, width)

    f1_piece = jnp.stack([t[:, :width] for t in head_totals])
    f2_piece = jnp.stack([t[:, width : width + longest] for t in head_totals])
    value_piece = jnp.concatenate([t[:, width + longest :] for t in head_totals], 1)
    return (
        result,
        input_grad,
        shared[0],
        shared[1],
        f1_piece,
        f1b_all,
        f2_piece,
        f2b_all,
        value_piece,
        out_piece,
        shared[2],
        shared[3],
        ffn_total[:, units:],
        upb_all,
        ffn_total[:, :units].T,
        shared[4],
    )


def solution(mesh):
    placed = (
        P(("dp", "head"), None),
        P("dp"),
        P(),
        P(),
        P("head", None, None),
        P("head", None),
        P("head", None, None),
        P("head", None),
        P(None, "head"),
        P(),
        P(),
        P(),
        P(None, "head"),
        P("head"),
        P("head", None),
        P(),
        P(("dp", "head"), None),
    )
    return jax.shard_map(
        local,
        mesh=mesh,
        in_specs=placed,
        out_specs=(
            P(("dp", "head"), None),
            P(("dp", "head"), None),
            P(),
            P(),
            P("head", "dp", None),
            P(),
            P("head", "dp", None),
            P(),
            P("dp", "head"),
            P("dp", None),
            P(),
            P(),
            P("dp", "head"),
            P(),
            P("head", "dp"),
            P(),
        ),
        check_vma=False,
    )
```

time: 1160 us -> 463 us (0.40)
  the two profiles are of different devices: /device:TPU:0 before, /device:TPU:12 now
where the time goes in v1:
time: 463 us; the launch traced here: 455 us
  waiting for transfers between devices  190 us (41%)
  Pallas kernels  160 us (35%)
  starting transfers between devices  42.8 us (9%)
  local copies, waits for them, and re-layouts  37.3 us (8%)
  other arithmetic  23.7 us (5%)
    ppermute x51, waiting for transfers between devices, swap(): lax.ppermute(value, axis, [(i, i ^ step) for i in range(lax.axis_size(axi...  190 us
    ppermute x51, starting transfers between devices, swap(): lax.ppermute(value, axis, [(i, i ^ step) for i in range(lax.axis_size(axi...  42.8 us
    pallas_call x3, Pallas kernels, head_back(): pl.pallas_call(head_back_kernel, grid=(slabs,), out_shape=[jax.ShapeDtype...  41.1 us
    pallas_call x4, Pallas kernels, head_forward(): pl.pallas_call(functools.partial(head_forward_kernel, step), grid=(heads,...  40.2 us
    unnamed x124, local copies, waits for them, and re-layouts  28.2 us
    pallas_call x4, Pallas kernels, input_term(): pl.pallas_call(functools.partial(input_term_kernel, heads), grid=(1,), ou...  23.6 us
    pallas_call x1, Pallas kernels, ffn_grads(): pl.pallas_call(functools.partial(ffn_grads_kernel, slabs), grid=(width //...  21.4 us
    pallas_call x4, Pallas kernels, ffn(): pl.pallas_call(ffn_kernel, out_shape=[jax.ShapeDtypeStruct(s, BF16) for s...  19.4 us
  transfers between devices with their start and end apart: 51, of which 24 were waited for; matrix products, arithmetic and copies ran while one was open for 7% of the time, Pallas kernels for 33%

profile of v1, /device:TPU:12, one launch (start us, length us, event | category | flops | bytes accessed | tf_op | source)
XLA Modules:
  0.0 455.0 jit_solution(12025247664021153876)
XLA Ops:
  5.0 15.2 %collective-permute-done.2.x_ref.refs_8_ = bf16[512,768]{1,0:T(8,128)(2,1)S(1)} collective-permute-done((bf16[512,768]{1,0:T(8,128)(2,1)}, bf16[512,768]{1,0:T(8,128)(2,1)S(1)}, u32[]{:S(2)}, u32[]{:S(2)}) %collective-permute-start.2) | collective-permute-done | bytes 786464 | tf_op jit(solution)/shard_map/ppermute | solution.py:48
  23.2 10.0 %head_forward.4 = (bf16[512,768]{1,0:T(8,128)(2,1)}, bf16[4,768,512]{2,1,0:T(8,128)(2,1)}, bf16[4,3,512,768]{3,2,1,0:T(8,128)(2,1)}, bf16[4,3,512,768]{3,2,1,0:T...) custom-call(s32[16]{0:T(128)S(1)} %copy-done.25, ...), custom_call_target="tpu_custom_call" | custom-call | flops 3321888768 | bytes 14680064 | tf_op jit(solution)/shard_map/head_forward/pallas_call | solution.py:160
  33.2 9.9 %head_forward.5 = (bf16[512,768]{1,0:T(8,128)(2,1)}, bf16[4,768,512]{2,1,0:T(8,128)(2,1)}, bf16[4,3,512,768]{3,2,1,0:T(8,128)(2,1)}, bf16[4,3,512,768]{3,2,1,0:T...) custom-call(s32[16]{0:T(128)S(1)} %copy-done.25, ...), custom_call_target="tpu_custom_call", output_to_operand_aliasing={{1}: (9, {}), {2}: (10, {}), {3}: (11, {}), {4}: (12, {}), ... | custom-call | flops 3321888768 | bytes 14680064 | tf_op jit(solution)/shard_map/head_forward/pallas_call | solution.py:160
  43.0 9.9 %head_forward.6 = (bf16[512,768]{1,0:T(8,128)(2,1)}, bf16[4,768,512]{2,1,0:T(8,128)(2,1)}, bf16[4,3,512,768]{3,2,1,0:T(8,128)(2,1)}, bf16[4,3,512,768]{3,2,1,0:T...) custom-call(s32[16]{0:T(128)S(1)} %copy-done.25, ...), custom_call_target="tpu_custom_call", output_to_operand_aliasing={{1}: (9, {}), {2}: (10, {}), {3}: (11, {}), {4}: (12, {}), ... | custom-call | flops 3321888768 | bytes 14680064 | tf_op jit(solution)/shard_map/head_forward/pallas_call | solution.py:160
  54.5 10.4 %head_forward.7 = (bf16[512,768]{1,0:T(8,128)(2,1)}, bf16[4,768,512]{2,1,0:T(8,128)(2,1)}, bf16[4,3,512,768]{3,2,1,0:T(8,128)(2,1)}, bf16[4,3,512,768]{3,2,1,0:T...) custom-call(s32[16]{0:T(128)S(1)} %copy-done.25, ...), custom_call_target="tpu_custom_call", output_to_operand_aliasing={{1}: (9, {}), {2}: (10, {}), {3}: (11, {}), {4}: (12, {}), ... | custom-call | flops 3321888768 | bytes 14680064 | tf_op jit(solution)/shard_map/head_forward/pallas_call | solution.py:160
  67.2 4.4 collective-permute-done.5.refs_3_
  77.1 12.7 %collective-permute-done.10.og_ref.refs_2_ = bf16[512,768]{1,0:T(8,128)(2,1)} collective-permute-done((bf16[512,768]{1,0:T(8,128)(2,1)S(1)}, bf16[512,768]{1,0:T(8,128)(2,1)}, u32[]{:S(2)}, u32[]{:S(2)}) %collective-permute-start.10) | collective-permute-done | bytes 786464 | tf_op jit(solution)/shard_map/ppermute | solution.py:48
  89.8 16.1 %collective-permute-done.9.n2_ref.refs_6_ = bf16[512,768]{1,0:T(8,128)(2,1)S(1)} collective-permute-done((bf16[512,768]{1,0:T(8,128)(2,1)S(1)}, bf16[512,768]{1,0:T(8,128)(2,1)S(1)}, u32[]{:S(2)}, u32[]{:S(2)}) %collective-permute-start.9) | collective-permute-done | bytes 786464 | tf_op jit(solution)/shard_map/ppermute | solution.py:48
  106.0 4.8 %ffn.4 = (bf16[512,768]{1,0:T(8,128)(2,1)S(1)}, bf16[512,768]{1,0:T(8,128)(2,1)S(1)}, bf16[512,768]{1,0:T(8,128)(2,1)S(1)}, bf16[512,768]{1,0:T(8,128)(2,1)S(1)}) custom-call(bf16[512,768]{1,0:T(8,128)(2,1)S(1)} %get-tuple-element.118.n2_ref.refs_4_, bf16[512,768]{1,0:T(8,128)(2,1)} %refs_0_, bf16[768,768]{1,0:T(8,128)(2,1)} %up_ref.7, ...), custom_call_target="tpu_custom_call" | custom-call | flops 2415919104 | bytes 7340032 | tf_op jit(solution)/shard_map/ffn/pallas_call | solution.py:218
  114.3 4.5 ffn.6
  122.4 4.8 %ffn.5 = (bf16[512,768]{1,0:T(8,128)(2,1)S(1)}, bf16[512,768]{1,0:T(8,128)(2,1)S(1)}, bf16[512,768]{1,0:T(8,128)(2,1)S(1)}, bf16[512,768]{1,0:T(8,128)(2,1)S(1)}) custom-call(bf16[512,768]{1,0:T(8,128)(2,1)S(1)} %collective-permute-done.6.n2_ref.refs_5_, bf16[512,768]{1,0:T(8,128)(2,1)} %copy-done.38, bf16[768,768]{1,0:T(8,128)(2,1)} %up_ref.7, ...), custom_call_target="tpu_custom_call" | custom-call | flops 2415919104 | bytes 7340032 | tf_op jit(solution)/shard_map/ffn/pallas_call | solution.py:218
  131.7 5.3 %ffn.7 = (bf16[512,768]{1,0:T(8,128)(2,1)}, bf16[512,768]{1,0:T(8,128)(2,1)S(1)}, bf16[512,768]{1,0:T(8,128)(2,1)S(1)}, bf16[512,768]{1,0:T(8,128)(2,1)S(1)}) custom-call(bf16[512,768]{1,0:T(8,128)(2,1)S(1)} %collective-permute-done.11.n2_ref.refs_7_, bf16[512,768]{1,0:T(8,128)(2,1)} %copy-done.41, bf16[768,768]{1,0:T(8,128)(2,1)} %up_ref.7, ...), custom_call_target="tpu_custom_call" | custom-call | flops 2415919104 | bytes 7340032 | tf_op jit(solution)/shard_map/ffn/pallas_call | solution.py:218
  141.1 21.4 %ffn_grads.1 = (bf16[4,96,1536]{2,1,0:T(8,128)(2,1)}, bf16[4,96,1536]{2,1,0:T(8,128)(2,1)}, f32[1,768]{1,0:T(1,128)S(1)}) custom-call(bf16[512,768]{1,0:T(8,128)(2,1)S(1)} %copy-done.15, bf16[512,768]{1,0:T(8,128)(2,1)S(1)} %copy-done.39, bf16[512,768]{1,0:T(8,128)(2,1)} %collective-permute-done.10.og_ref.refs_2_, bf16[512,768]{1,0:T(8,128)(2,1)S(1)} %copy-done.42, ...), custom_call_target="tpu_custom_call" | custom-call | flops 4831838208 | bytes 18874368 | tf_op jit(solution)/shard_map/ffn_grads/pallas_call | solution.py:270
  166.5 24.4 %collective-permute-done.47 = bf16[4,96,1536]{2,1,0:T(8,128)(2,1)} collective-permute-done((bf16[4,96,1536]{2,1,0:T(8,128)(2,1)}, bf16[4,96,1536]{2,1,0:T(8,128)(2,1)}, u32[]{:S(2)}, u32[]{:S(2)}) %collective-permute-start.47) | collective-permute-done | bytes 1179680 | tf_op jit(solution)/shard_map/ppermute | solution.py:48
  194.5 5.2 %residual_back.1 = (f32[512,768]{1,0:T(8,128)}, bf16[512,768]{1,0:T(8,128)(2,1)S(1)}, f32[3,768]{1,0:T(4,128)S(1)}, bf16[192,512]{1,0:T(8,128)(2,1)S(1)}, bf16[1...) custom-call(bf16[512,768]{1,0:T(8,128)(2,1)S(1)} %copy-done.19, ...), custom_call_target="tpu_custom_call" | custom-call | flops 603979776 | bytes 9437184 | tf_op jit(solution)/shard_map/residual_back/pallas_call | solution.py:309
  203.8 4.6 %collective-permute-done.19 = bf16[192,512]{1,0:T(8,128)(2,1)S(1)} collective-permute-done((bf16[192,512]{1,0:T(8,128)(2,1)}, bf16[192,512]{1,0:T(8,128)(2,1)S(1)}, u32[]{:S(2)}, u32[]{:S(2)}) %collective-permute-start.19) | collective-permute-done | bytes 196640 | tf_op jit(solution)/shard_map/ppermute | solution.py:48
  213.5 13.9 %head_back.3 = (bf16[4,512,768]{2,1,0:T(8,128)(2,1)}, bf16[4,64,512]{2,1,0:T(8,128)(2,1)S(1)}, f32[1,768]{1,0:T(1,128)S(1)}, f32[1,512]{1,0:T(1,128)S(1)}, bf16[...) custom-call(s32[16]{0:T(128)S(1)} %copy-done.26, bf16[4,3,512,512]{3,2,1,0:T(8,128)(2,1)} %get-tuple-element.124.prob_ref, ...), custom_call_target="tpu_custom_call" | custom-call | flops 6442450944 | bytes 20971520 | tf_op jit(solution)/shard_map/head_back/pallas_call | solution.py:425
  228.4 13.5 %head_back.4 = (bf16[4,512,768]{2,1,0:T(8,128)(2,1)}, bf16[4,64,512]{2,1,0:T(8,128)(2,1)S(1)}, f32[1,768]{1,0:T(1,128)S(1)}, f32[1,512]{1,0:T(1,128)S(1)}, bf16[...) custom-call(s32[16]{0:T(128)S(1)} %copy-done.26, bf16[4,3,512,512]{3,2,1,0:T(8,128)(2,1)} %get-tuple-element.124.prob_ref, ...), custom_call_target="tpu_custom_call" | custom-call | flops 6442450944 | bytes 20971520 | tf_op jit(solution)/shard_map/head_back/pallas_call | solution.py:425
  244.0 13.7 %head_back.5 = (bf16[4,512,768]{2,1,0:T(8,128)(2,1)}, bf16[4,64,512]{2,1,0:T(8,128)(2,1)S(1)}, f32[1,768]{1,0:T(1,128)S(1)}, f32[1,512]{1,0:T(1,128)S(1)}, bf16[...) custom-call(s32[16]{0:T(128)S(1)} %copy-done.26, bf16[4,3,512,512]{3,2,1,0:T(8,128)(2,1)} %get-tuple-element.124.prob_ref, ...), custom_call_target="tpu_custom_call" | custom-call | flops 6442450944 | bytes 20971520 | tf_op jit(solution)/shard_map/head_back/pallas_call | solution.py:425
  260.9 6.6 %input_term.4 = (bf16[512,768]{1,0:T(8,128)(2,1)}, f32[2,768]{1,0:T(2,128)S(1)}) custom-call(bf16[4,512,768]{2,1,0:T(8,128)(2,1)} %get-tuple-element.137.refs_0_, bf16[4,512,768]{2,1,0:T(8,128)(2,1)} %get-tuple-element.138.refs_1_, bf16[4,512,768]{2,1,0:T(8,128)(2,1)} %get-tuple-element.139.refs_2_, bf16[4,64,512]{2,1,0:T(8,128)(2,1)S(1)} %get-tuple-element.140.refs_3_, ...), custom_call_target="tpu_custom_call" | custom-call | flops 2415919104 | bytes 8388608 | tf_op jit(solution)/shard_map/input_term/pallas_call | solution.py:487
  267.4 5.6 %input_term.5 = (bf16[512,768]{1,0:T(8,128)(2,1)S(1)}, f32[2,768]{1,0:T(2,128)S(1)}) custom-call(bf16[4,512,768]{2,1,0:T(8,128)(2,1)} %get-tuple-element.137.refs_0_, bf16[4,512,768]{2,1,0:T(8,128)(2,1)} %get-tuple-element.138.refs_1_, bf16[4,512,768]{2,1,0:T(8,128)(2,1)} %get-tuple-element.139.refs_2_, bf16[4,64,512]{2,1,0:T(8,128)(2,1)S(1)} %get-tuple-element.140.refs_3_, ...), custom_call_target="tpu_custom_call" | custom-call | flops 2415919104 | bytes 8388608 | tf_op jit(solution)/shard_map/input_term/pallas_call | solution.py:487
  274.0 5.6 %input_term.6 = (bf16[512,768]{1,0:T(8,128)(2,1)S(1)}, f32[2,768]{1,0:T(2,128)S(1)}) custom-call(bf16[4,512,768]{2,1,0:T(8,128)(2,1)} %get-tuple-element.137.refs_0_, bf16[4,512,768]{2,1,0:T(8,128)(2,1)} %get-tuple-element.138.refs_1_, bf16[4,512,768]{2,1,0:T(8,128)(2,1)} %get-tuple-element.139.refs_2_, bf16[4,64,512]{2,1,0:T(8,128)(2,1)S(1)} %get-tuple-element.140.refs_3_, ...), custom_call_target="tpu_custom_call" | custom-call | flops 2415919104 | bytes 8388608 | tf_op jit(solution)/shard_map/input_term/pallas_call | solution.py:487
  280.5 5.7 %input_term.7 = (bf16[512,768]{1,0:T(8,128)(2,1)S(1)}, f32[2,768]{1,0:T(2,128)S(1)}) custom-call(bf16[4,512,768]{2,1,0:T(8,128)(2,1)} %get-tuple-element.137.refs_0_, bf16[4,512,768]{2,1,0:T(8,128)(2,1)} %get-tuple-element.138.refs_1_, bf16[4,512,768]{2,1,0:T(8,128)(2,1)} %get-tuple-element.139.refs_2_, bf16[4,64,512]{2,1,0:T(8,128)(2,1)S(1)} %get-tuple-element.140.refs_3_, ...), custom_call_target="tpu_custom_call" | custom-call | flops 2415919104 | bytes 8388608 | tf_op jit(solution)/shard_map/input_term/pallas_call | solution.py:487
  304.5 5.5 %collective-permute-done.14 = bf16[512,768]{1,0:T(8,128)(2,1)} collective-permute-done((bf16[512,768]{1,0:T(8,128)(2,1)}, bf16[512,768]{1,0:T(8,128)(2,1)}, u32[]{:S(2)}, u32[]{:S(2)}) %collective-permute-start.14) | collective-permute-done | bytes 786464 | tf_op jit(solution)/shard_map/ppermute | solution.py:48
  314.5 4.2 collective-permute-done.41
  329.2 5.3 %collective-permute-done.43 = bf16[96,768]{1,0:T(8,128)(2,1)S(1)} collective-permute-done((bf16[96,768]{1,0:T(8,128)(2,1)}, bf16[96,768]{1,0:T(8,128)(2,1)S(1)}, u32[]{:S(2)}, u32[]{:S(2)}) %collective-permute-start.43) | collective-permute-done | bytes 147488 | tf_op jit(solution)/shard_map/ppermute | solution.py:48
  350.9 14.1 %collective-permute-done.33 = bf16[4,96,1344]{2,1,0:T(8,128)(2,1)S(1)} collective-permute-done((bf16[4,96,1344]{2,1,0:T(8,128)(2,1)}, bf16[4,96,1344]{2,1,0:T(8,128)(2,1)S(1)}, u32[]{:S(2)}, u32[]{:S(2)}) %collective-permute-start.33) | collective-permute-done | bytes 1032224 | tf_op jit(solution)/shard_map/ppermute | solution.py:48
  366.1 21.7 %collective-permute-done.37 = bf16[4,96,1344]{2,1,0:T(8,128)(2,1)S(1)} collective-permute-done((bf16[4,96,1344]{2,1,0:T(8,128)(2,1)}, bf16[4,96,1344]{2,1,0:T(8,128)(2,1)S(1)}, u32[]{:S(2)}, u32[]{:S(2)}) %collective-permute-start.37) | collective-permute-done | bytes 1032224 | tf_op jit(solution)/shard_map/ppermute | solution.py:48
  392.6 10.5 %collective-permute-done.32 = bf16[96,1344]{1,0:T(8,128)(2,1)S(1)} collective-permute-done((bf16[96,1344]{1,0:T(8,128)(2,1)S(1)}, bf16[96,1344]{1,0:T(8,128)(2,1)S(1)}, u32[]{:S(2)}, u32[]{:S(2)}) %collective-permute-start.32) | collective-permute-done | bytes 258080 | tf_op jit(solution)/shard_map/ppermute | solution.py:48
  406.1 12.3 %collective-permute-done.35 = bf16[96,1344]{1,0:T(8,128)(2,1)S(1)} collective-permute-done((bf16[96,1344]{1,0:T(8,128)(2,1)S(1)}, bf16[96,1344]{1,0:T(8,128)(2,1)S(1)}, u32[]{:S(2)}, u32[]{:S(2)}) %collective-permute-start.35) | collective-permute-done | bytes 258080 | tf_op jit(solution)/shard_map/ppermute | solution.py:48
  421.8 15.9 %collective-permute-done.36 = bf16[96,1344]{1,0:T(8,128)(2,1)S(1)} collective-permute-done((bf16[96,1344]{1,0:T(8,128)(2,1)S(1)}, bf16[96,1344]{1,0:T(8,128)(2,1)S(1)}, u32[]{:S(2)}, u32[]{:S(2)}) %collective-permute-start.36) | collective-permute-done | bytes 258080 | tf_op jit(solution)/shard_map/ppermute | solution.py:48
  441.6 6.4 %collective-permute-done.40 = bf16[96,1344]{1,0:T(8,128)(2,1)S(1)} collective-permute-done((bf16[96,1344]{1,0:T(8,128)(2,1)S(1)}, bf16[96,1344]{1,0:T(8,128)(2,1)S(1)}, u32[]{:S(2)}, u32[]{:S(2)}) %collective-permute-start.40) | collective-permute-done | bytes 258080 | tf_op jit(solution)/shard_map/ppermute | solution.py:48
  (288 shorter events, 129.2 us)
Async XLA Ops:
  0.6 19.6 %collective-permute-start.2 = (bf16[512,768]{1,0:T(8,128)(2,1)}, bf16[512,768]{1,0:T(8,128)(2,1)S(1)}, u32[]{:S(2)}, u32[]{:S(2)}) collective-permute-start(bf16[512,768]{1,0:T(8,128)(2,1)} %x_ref.3), channel_id=1, source_target_pairs={{0,2},{1,3},{2,0},{3,1},{4,6},{5,7},{6,4},{7,5},{8,10},{9,11},{10,... | collective-permute-start | bytes 2359304 | tf_op jit(solution)/shard_map/ppermute | solution.py:48
  2.2 31.0 %collective-permute-start = (bf16[512,768]{1,0:T(8,128)(2,1)}, bf16[512,768]{1,0:T(8,128)(2,1)S(1)}, u32[]{:S(2)}, u32[]{:S(2)}) collective-permute-start(bf16[512,768]{1,0:T(8,128)(2,1)} %x_ref.3), channel_id=1, source_target_pairs={{0,1},{1,0},{2,3},{3,2},{4,5},{5,4},{6,7},{7,6},{8,9},{9,8},{10,11... | collective-permute-start | bytes 2359304 | tf_op jit(solution)/shard_map/ppermute | solution.py:48
  20.2 34.3 %collective-permute-start.4 = (bf16[512,768]{1,0:T(8,128)(2,1)S(1)}, bf16[512,768]{1,0:T(8,128)(2,1)S(1)}, u32[]{:S(2)}, u32[]{:S(2)}) collective-permute-start(bf16[512,768]{1,0:T(8,128)(2,1)S(1)} %collective-permute-done.2.x_ref.refs_8_), channel_id=1, source_target_pairs={{0,1},{1,0},{2,3},{3,2},{4,5},{5,4},{6,7},{7,6},{8,9},{9,8},{10,11... | collective-permute-start | bytes 2359304 | tf_op jit(solution)/shard_map/ppermute | solution.py:48
  65.6 24.2 %collective-permute-start.10 = (bf16[512,768]{1,0:T(8,128)(2,1)S(1)}, bf16[512,768]{1,0:T(8,128)(2,1)}, u32[]{:S(2)}, u32[]{:S(2)}) collective-permute-start(bf16[512,768]{1,0:T(8,128)(2,1)S(1)} %copy-done.14), channel_id=1, source_target_pairs={{0,2},{1,3},{2,0},{3,1},{4,6},{5,7},{6,4},{7,5},{8,10},{9,11},{10,... | collective-permute-start | bytes 2359304 | tf_op jit(solution)/shard_map/ppermute | solution.py:48
  75.9 30.1 %collective-permute-start.9 = (bf16[512,768]{1,0:T(8,128)(2,1)S(1)}, bf16[512,768]{1,0:T(8,128)(2,1)S(1)}, u32[]{:S(2)}, u32[]{:S(2)}) collective-permute-start(bf16[512,768]{1,0:T(8,128)(2,1)S(1)} %get-tuple-element.118.n2_ref.refs_4_), channel_id=1, source_target_pairs={{0,2},{1,3},{2,0},{3,1},{4,6},{5,7},{6,4},{7,5},{8,10},{9,11},{10,... | collective-permute-start | bytes 2359304 | tf_op jit(solution)/shard_map/ppermute | solution.py:48
  76.6 44.9 %collective-permute-start.7 = (bf16[512,768]{1,0:T(8,128)(2,1)S(1)}, bf16[512,768]{1,0:T(8,128)(2,1)S(1)}, u32[]{:S(2)}, u32[]{:S(2)}) collective-permute-start(bf16[512,768]{1,0:T(8,128)(2,1)S(1)} %copy-done.14), channel_id=1, source_target_pairs={{0,1},{1,0},{2,3},{3,2},{4,5},{5,4},{6,7},{7,6},{8,9},{9,8},{10,11... | collective-permute-start | bytes 2359304 | tf_op jit(solution)/shard_map/ppermute | solution.py:48
  77.1 44.4 %collective-permute-start.6 = (bf16[512,768]{1,0:T(8,128)(2,1)S(1)}, bf16[512,768]{1,0:T(8,128)(2,1)S(1)}, u32[]{:S(2)}, u32[]{:S(2)}) collective-permute-start(bf16[512,768]{1,0:T(8,128)(2,1)S(1)} %get-tuple-element.118.n2_ref.refs_4_), channel_id=1, source_target_pairs={{0,1},{1,0},{2,3},{3,2},{4,5},{5,4},{6,7},{7,6},{8,9},{9,8},{10,11... | collective-permute-start | bytes 2359304 | tf_op jit(solution)/shard_map/ppermute | solution.py:48
  89.8 41.1 %collective-permute-start.12 = (bf16[512,768]{1,0:T(8,128)(2,1)}, bf16[512,768]{1,0:T(8,128)(2,1)S(1)}, u32[]{:S(2)}, u32[]{:S(2)}) collective-permute-start(bf16[512,768]{1,0:T(8,128)(2,1)} %collective-permute-done.10.og_ref.refs_2_), channel_id=1, source_target_pairs={{0,1},{1,0},{2,3},{3,2},{4,5},{5,4},{6,7},{7,6},{8,9},{9,8},{10,11... | collective-permute-start | bytes 2359304 | tf_op jit(solution)/shard_map/ppermute | solution.py:48
  105.9 24.9 %collective-permute-start.11 = (bf16[512,768]{1,0:T(8,128)(2,1)S(1)}, bf16[512,768]{1,0:T(8,128)(2,1)S(1)}, u32[]{:S(2)}, u32[]{:S(2)}) collective-permute-start(bf16[512,768]{1,0:T(8,128)(2,1)S(1)} %collective-permute-done.9.n2_ref.refs_6_), channel_id=1, source_target_pairs={{0,1},{1,0},{2,3},{3,2},{4,5},{5,4},{6,7},{7,6},{8,9},{9,8},{10,11... | collective-permute-start | bytes 2359304 | tf_op jit(solution)/shard_map/ppermute | solution.py:48
  139.7 23.2 %collective-permute-start.16 = (bf16[512,768]{1,0:T(8,128)(2,1)}, bf16[512,768]{1,0:T(8,128)(2,1)}, u32[]{:S(2)}, u32[]{:S(2)}) collective-permute-start(bf16[512,768]{1,0:T(8,128)(2,1)} %get-tuple-element.129), channel_id=1, source_target_pairs={{0,1},{1,0},{2,3},{3,2},{4,5},{5,4},{6,7},{7,6},{8,9},{9,8},{10,11... | collective-permute-start | bytes 2359304 | tf_op jit(solution)/shard_map/ppermute | solution.py:48
  162.4 28.5 %collective-permute-start.47 = (bf16[4,96,1536]{2,1,0:T(8,128)(2,1)}, bf16[4,96,1536]{2,1,0:T(8,128)(2,1)}, u32[]{:S(2)}, u32[]{:S(2)}) collective-permute-start(bf16[4,96,1536]{2,1,0:T(8,128)(2,1)} %get-tuple-element.179), channel_id=1, source_target_pairs={{0,4},{4,0},{8,12},{12,8},{16,20},{20,16},{24,28},{28,24},{1,5},{5... | collective-permute-start | bytes 3538952 | tf_op jit(solution)/shard_map/ppermute | solution.py:48
  162.9 31.6 %collective-permute-start.15 = (bf16[512,768]{1,0:T(8,128)(2,1)}, bf16[512,768]{1,0:T(8,128)(2,1)S(1)}, u32[]{:S(2)}, u32[]{:S(2)}) collective-permute-start(bf16[512,768]{1,0:T(8,128)(2,1)} %copy-done.36), channel_id=1, source_target_pairs={{0,1},{1,0},{2,3},{3,2},{4,5},{5,4},{6,7},{7,6},{8,9},{9,8},{10,11... | collective-permute-start | bytes 2359304 | tf_op jit(solution)/shard_map/ppermute | solution.py:48
  165.4 29.1 %collective-permute-start.17 = (bf16[512,768]{1,0:T(8,128)(2,1)}, bf16[512,768]{1,0:T(8,128)(2,1)}, u32[]{:S(2)}, u32[]{:S(2)}) collective-permute-start(bf16[512,768]{1,0:T(8,128)(2,1)} %add_convert_fusion.1), channel_id=1, source_target_pairs={{0,2},{1,3},{2,0},{3,1},{4,6},{5,7},{6,4},{7,5},{8,10},{9,11},{10,... | collective-permute-start | bytes 2359304 | tf_op jit(solution)/shard_map/ppermute | solution.py:48
  165.9 138.6 %collective-permute-start.8 = (bf16[512,768]{1,0:T(8,128)(2,1)}, bf16[512,768]{1,0:T(8,128)(2,1)}, u32[]{:S(2)}, u32[]{:S(2)}) collective-permute-start(bf16[512,768]{1,0:T(8,128)(2,1)} %copy-done.32), channel_id=1, source_target_pairs={{0,1},{1,0},{2,3},{3,2},{4,5},{5,4},{6,7},{7,6},{8,9},{9,8},{10,11... | collective-permute-start | bytes 2359304 | tf_op jit(solution)/shard_map/ppermute | solution.py:48
  166.2 120.2 %collective-permute-start.13 = (bf16[512,768]{1,0:T(8,128)(2,1)}, bf16[512,768]{1,0:T(8,128)(2,1)}, u32[]{:S(2)}, u32[]{:S(2)}) collective-permute-start(bf16[512,768]{1,0:T(8,128)(2,1)} %copy-done.33), channel_id=1, source_target_pairs={{0,1},{1,0},{2,3},{3,2},{4,5},{5,4},{6,7},{7,6},{8,9},{9,8},{10,11... | collective-permute-start | bytes 2359304 | tf_op jit(solution)/shard_map/ppermute | solution.py:48
  203.3 87.7 %collective-permute-start.48 = (bf16[96,1536]{1,0:T(8,128)(2,1)}, bf16[96,1536]{1,0:T(8,128)(2,1)}, u32[]{:S(2)}, u32[]{:S(2)}) collective-permute-start(bf16[96,1536]{1,0:T(8,128)(2,1)} %get-tuple-element.188), channel_id=1, source_target_pairs={{0,8},{4,12},{8,0},{12,4},{16,24},{20,28},{24,16},{28,20},{1,9},{5... | collective-permute-start | bytes 884744 | tf_op jit(solution)/shard_map/ppermute | solution.py:48
  208.4 85.1 %collective-permute-start.49 = (bf16[96,1536]{1,0:T(8,128)(2,1)}, bf16[96,1536]{1,0:T(8,128)(2,1)}, u32[]{:S(2)}, u32[]{:S(2)}) collective-permute-start(bf16[96,1536]{1,0:T(8,128)(2,1)} %get-tuple-element.190), channel_id=1, source_target_pairs={{0,16},{4,20},{8,24},{12,28},{16,0},{20,4},{24,8},{28,12},{1,17},{... | collective-permute-start | bytes 884744 | tf_op jit(solution)/shard_map/ppermute | solution.py:48
  211.9 81.7 %collective-permute-start.50 = (bf16[96,1536]{1,0:T(8,128)(2,1)}, bf16[96,1536]{1,0:T(8,128)(2,1)}, u32[]{:S(2)}, u32[]{:S(2)}) collective-permute-start(bf16[96,1536]{1,0:T(8,128)(2,1)} %get-tuple-element.189), channel_id=1, source_target_pairs={{0,24},{4,28},{8,16},{12,20},{16,8},{20,12},{24,0},{28,4},{1,25},{... | collective-permute-start | bytes 884744 | tf_op jit(solution)/shard_map/ppermute | solution.py:48
  290.4 19.5 %collective-permute-start.14 = (bf16[512,768]{1,0:T(8,128)(2,1)}, bf16[512,768]{1,0:T(8,128)(2,1)}, u32[]{:S(2)}, u32[]{:S(2)}) collective-permute-start(bf16[512,768]{1,0:T(8,128)(2,1)} %add_convert_fusion.2), channel_id=1, source_target_pairs={{0,2},{1,3},{2,0},{3,1},{4,6},{5,7},{6,4},{7,5},{8,10},{9,11},{10,... | collective-permute-start | bytes 2359304 | tf_op jit(solution)/shard_map/ppermute | solution.py:48
  302.3 16.4 %collective-permute-start.41 = (bf16[4,96,768]{2,1,0:T(8,128)(2,1)}, bf16[4,96,768]{2,1,0:T(8,128)(2,1)}, u32[]{:S(2)}, u32[]{:S(2)}) collective-permute-start(bf16[4,96,768]{2,1,0:T(8,128)(2,1)} %get-tuple-element.177), channel_id=1, source_target_pairs={{0,4},{4,0},{8,12},{12,8},{16,20},{20,16},{24,28},{28,24},{1,5},{5... | collective-permute-start | bytes 1769480 | tf_op jit(solution)/shard_map/ppermute | solution.py:48
  313.3 35.7 %collective-permute-start.29 = (bf16[4,96,1344]{2,1,0:T(8,128)(2,1)}, bf16[4,96,1344]{2,1,0:T(8,128)(2,1)}, u32[]{:S(2)}, u32[]{:S(2)}) collective-permute-start(bf16[4,96,1344]{2,1,0:T(8,128)(2,1)} %get-tuple-element.169), channel_id=1, source_target_pairs={{0,4},{4,0},{8,12},{12,8},{16,20},{20,16},{24,28},{28,24},{1,5},{5... | collective-permute-start | bytes 3096584 | tf_op jit(solution)/shard_map/ppermute | solution.py:48
  314.4 26.1 %collective-permute-start.22 = (bf16[512,768]{1,0:T(8,128)(2,1)}, bf16[512,768]{1,0:T(8,128)(2,1)}, u32[]{:S(2)}, u32[]{:S(2)}) collective-permute-start(bf16[512,768]{1,0:T(8,128)(2,1)} %get-tuple-element.149), channel_id=1, source_target_pairs={{0,1},{1,0},{2,3},{3,2},{4,5},{5,4},{6,7},{7,6},{8,9},{9,8},{10,11... | collective-permute-start | bytes 2359304 | tf_op jit(solution)/shard_map/ppermute | solution.py:48
  328.7 36.3 %collective-permute-start.33 = (bf16[4,96,1344]{2,1,0:T(8,128)(2,1)}, bf16[4,96,1344]{2,1,0:T(8,128)(2,1)S(1)}, u32[]{:S(2)}, u32[]{:S(2)}) collective-permute-start(bf16[4,96,1344]{2,1,0:T(8,128)(2,1)} %copy-done.28), channel_id=1, source_target_pairs={{0,4},{4,0},{8,12},{12,8},{16,20},{20,16},{24,28},{28,24},{1,5},{5... | collective-permute-start | bytes 3096584 | tf_op jit(solution)/shard_map/ppermute | solution.py:48
  334.5 53.2 %collective-permute-start.37 = (bf16[4,96,1344]{2,1,0:T(8,128)(2,1)}, bf16[4,96,1344]{2,1,0:T(8,128)(2,1)S(1)}, u32[]{:S(2)}, u32[]{:S(2)}) collective-permute-start(bf16[4,96,1344]{2,1,0:T(8,128)(2,1)} %copy-done.27), channel_id=1, source_target_pairs={{0,4},{4,0},{8,12},{12,8},{16,20},{20,16},{24,28},{28,24},{1,5},{5... | collective-permute-start | bytes 3096584 | tf_op jit(solution)/shard_map/ppermute | solution.py:48
  340.4 110.4 %collective-permute-start.21 = (bf16[512,768]{1,0:T(8,128)(2,1)}, bf16[512,768]{1,0:T(8,128)(2,1)S(1)}, u32[]{:S(2)}, u32[]{:S(2)}) collective-permute-start(bf16[512,768]{1,0:T(8,128)(2,1)} %copy-done.29), channel_id=1, source_target_pairs={{0,1},{1,0},{2,3},{3,2},{4,5},{5,4},{6,7},{7,6},{8,9},{9,8},{10,11... | collective-permute-start | bytes 2359304 | tf_op jit(solution)/shard_map/ppermute | solution.py:48
  346.8 104.1 %collective-permute-start.23 = (bf16[512,768]{1,0:T(8,128)(2,1)S(1)}, bf16[512,768]{1,0:T(8,128)(2,1)S(1)}, u32[]{:S(2)}, u32[]{:S(2)}) collective-permute-start(bf16[512,768]{1,0:T(8,128)(2,1)S(1)} %add_convert_fusion), channel_id=1, source_target_pairs={{0,2},{1,3},{2,0},{3,1},{4,6},{5,7},{6,4},{7,5},{8,10},{9,11},{10,... | collective-permute-start | bytes 2359304 | tf_op jit(solution)/shard_map/ppermute | solution.py:48
  350.6 38.1 %collective-permute-start.30 = (bf16[96,1344]{1,0:T(8,128)(2,1)S(1)}, bf16[96,1344]{1,0:T(8,128)(2,1)S(1)}, u32[]{:S(2)}, u32[]{:S(2)}) collective-permute-start(bf16[96,1344]{1,0:T(8,128)(2,1)S(1)} %get-tuple-element.193), channel_id=1, source_target_pairs={{0,8},{4,12},{8,0},{12,4},{16,24},{20,28},{24,16},{28,20},{1,9},{5... | collective-permute-start | bytes 774152 | tf_op jit(solution)/shard_map/ppermute | solution.py:48
  365.0 25.4 %collective-permute-start.31 = (bf16[96,1344]{1,0:T(8,128)(2,1)S(1)}, bf16[96,1344]{1,0:T(8,128)(2,1)S(1)}, u32[]{:S(2)}, u32[]{:S(2)}) collective-permute-start(bf16[96,1344]{1,0:T(8,128)(2,1)S(1)} %get-tuple-element.195), channel_id=1, source_target_pairs={{0,16},{4,20},{8,24},{12,28},{16,0},{20,4},{24,8},{28,12},{1,17},{... | collective-permute-start | bytes 774152 | tf_op jit(solution)/shard_map/ppermute | solution.py:48
  390.3 28.1 %collective-permute-start.35 = (bf16[96,1344]{1,0:T(8,128)(2,1)S(1)}, bf16[96,1344]{1,0:T(8,128)(2,1)S(1)}, u32[]{:S(2)}, u32[]{:S(2)}) collective-permute-start(bf16[96,1344]{1,0:T(8,128)(2,1)S(1)} %get-tuple-element.198), channel_id=1, source_target_pairs={{0,16},{4,20},{8,24},{12,28},{16,0},{20,4},{24,8},{28,12},{1,17},{... | collective-permute-start | bytes 774152 | tf_op jit(solution)/shard_map/ppermute | solution.py:48
  403.1 34.6 %collective-permute-start.36 = (bf16[96,1344]{1,0:T(8,128)(2,1)S(1)}, bf16[96,1344]{1,0:T(8,128)(2,1)S(1)}, u32[]{:S(2)}, u32[]{:S(2)}) collective-permute-start(bf16[96,1344]{1,0:T(8,128)(2,1)S(1)} %get-tuple-element.197), channel_id=1, source_target_pairs={{0,24},{4,28},{8,16},{12,20},{16,8},{20,12},{24,0},{28,4},{1,25},{... | collective-permute-start | bytes 774152 | tf_op jit(solution)/shard_map/ppermute | solution.py:48
  404.8 33.7 %collective-permute-start.38 = (bf16[96,1344]{1,0:T(8,128)(2,1)S(1)}, bf16[96,1344]{1,0:T(8,128)(2,1)S(1)}, u32[]{:S(2)}, u32[]{:S(2)}) collective-permute-start(bf16[96,1344]{1,0:T(8,128)(2,1)S(1)} %get-tuple-element.199), channel_id=1, source_target_pairs={{0,8},{4,12},{8,0},{12,4},{16,24},{20,28},{24,16},{28,20},{1,9},{5... | collective-permute-start | bytes 774152 | tf_op jit(solution)/shard_map/ppermute | solution.py:48
  418.4 23.2 %collective-permute-start.39 = (bf16[96,1344]{1,0:T(8,128)(2,1)S(1)}, bf16[96,1344]{1,0:T(8,128)(2,1)S(1)}, u32[]{:S(2)}, u32[]{:S(2)}) collective-permute-start(bf16[96,1344]{1,0:T(8,128)(2,1)S(1)} %get-tuple-element.201), channel_id=1, source_target_pairs={{0,16},{4,20},{8,24},{12,28},{16,0},{20,4},{24,8},{28,12},{1,17},{... | collective-permute-start | bytes 774152 | tf_op jit(solution)/shard_map/ppermute | solution.py:48
  (75 other events, 505.8 us)
